TPU v7x, 256 devices: a whole 4x4x8 slice. The times are simulated.
256 devices in a mesh: rows: 32 (over x, y, core), blk: 8 (over z).
Axes of the slice: x: 4, y: 4, z: 8, core: 2. Of those that a mesh axis runs over, the one named last changes fastest.
Arguments:
- amplitudes: float32 [256, 160000], P('rows', 'blk'), may hold values from -6 to 6
- pair_irrep: int32 [256], P('rows'), may hold values from 0 to 7
- virt_irrep: int32 [400], replicated, may hold values from 0 to 7, as said below
- resid_in: float32 [256, 4864], P('blk', 'rows'), may hold values from -4 to 4
- ladder_ints: float32 [4864, 160000], P('rows', 'blk'), may hold values from -0.0390625 to 0.0390625
Outputs:
- residual: float32 [256, 4864], P('blk', 'rows')
Inputs may be any that keep to these rules, and one draw needn't show every extreme that they name: `virt_irrep`: each of the 8 irreps labels exactly 50 virtual orbitals.
All inputs are finite; a program needn't handle non-finite values.
Results may differ from a plain program's by a relative error of at most 0.0001.
Values sent between devices are 32-bit elements; how exact they have to be, the bound alone decides.
No kernel may reach another device: no remote copies, remote signals or barrier semaphores. Data moves between devices by JAX's collectives and lax.ppermute only.
A program may use at most 128 MiB of HBM per device.

v0:
```python
import jax
import jax.numpy as jnp
from jax import lax
from jax.sharding import PartitionSpec as P


def body(amplitudes, pair_irrep, virt_irrep, resid_in, ladder_ints):
    panel_cols = amplitudes.shape[1]
    nvirt = virt_irrep.shape[0]
    c_count = panel_cols // nvirt
    first_irrep = lax.dynamic_slice_in_dim(virt_irrep, lax.axis_index("blk") * c_count, c_count, 0)
    sector = jnp.bitwise_xor(first_irrep[:, None], virt_irrep[None, :]).reshape(panel_cols)
    allowed = jnp.where(
        sector[None, :] == pair_irrep[:, None], amplitudes, jnp.zeros_like(amplitudes)
    )
    whole = lax.all_gather(allowed, "rows", axis=0, tiled=True)
    terms = lax.dot_general(
        whole,
        ladder_ints,
        (((1,), (1,)), ((), ())),
        precision=lax.Precision.HIGHEST,
        preferred_element_type=jnp.float32,
    )
    ladder = lax.psum_scatter(terms, "blk", scatter_dimension=0, tiled=True)
    return resid_in + ladder


def solution(mesh):
    placed = (P("rows", "blk"), P("rows"), P(), P("blk", "rows"), P("rows", "blk"))
    return jax.shard_map(
        body, mesh=mesh, in_specs=placed, out_specs=P("blk", "rows"), check_vma=False
    )
```

profile of v0, /device:TPU:6, one launch (start us, length us, event | category | flops | bytes accessed | tf_op | source)
XLA Modules:
  0.0 165.7 jit_solution(5884584422887024716)
XLA Ops:
  6.5 0.0 all-gather.2.cloned.1.call-start
  6.5 0.8 dynamic_slice.3
  7.3 0.8 broadcast_xor_fusion
  8.0 0.1 xor.23
  8.2 2.1 %compare_select_fusion = f32[8,20000]{1,0:T(8,128)} fusion(f32[8,20000]{1,0:T(8,128)} %param.5, s32[20000]{0:T(1024)S(1)} %xor.23, s32[8]{0:T(128)} %param.6), kind=kLoop, calls=%fused_computation | loop fusion | flops 320000 | bytes 1360032 | tf_op jit(solution)/shard_map/jit(_where)/select_n | solution.py:13
  10.2 0.0 all-gather.2.cloned.1.call-update
  10.3 0.0 copy-start
  10.3 0.0 reduce-scatter.2.cloned.1.call-start
  10.3 89.6 %all-gather.2.cloned.1.call-done = f32[256,20000]{1,0:T(8,128)} async-done(((f32[8,20000]{1,0:T(8,128)}), f32[256,20000]{1,0:T(8,128)}) %all-gather.2.cloned.1.call-update) | async-done | bytes 20480016 | tf_op jit(solution)/shard_map/all_gather | solution.py:16
  99.9 21.2 %fusion = f32[256,152]{1,0:T(8,128)} fusion(f32[256,20000]{1,0:T(8,128)} %all-gather.2.cloned.1.call-done, f32[152,20000]{1,0:T(8,128)} %param.9), kind=kOutput, calls=%fused_computation.2 | convolution fusion | flops 9338880000 | bytes 32795648 | tf_op jit(solution)/shard_map/dot_general | solution.py:17
  121.1 0.0 reduce-scatter.2.cloned.1.call-update
  121.1 36.4 %reduce-scatter.2.cloned.1.call-done = f32[32,152]{1,0:T(8,128)} async-done(((f32[256,152]{1,0:T(8,128)}), f32[32,152]{1,0:T(8,128)}) %reduce-scatter.2.cloned.1.call-update) | async-done | bytes 19472 | tf_op jit(solution)/shard_map/reduce_scatter | solution.py:24
  157.5 0.0 copy-done
  157.5 1.4 add.9
Async XLA Ops:
  6.5 93.3 %all-gather.2.cloned.1.call-start = ((), (), s32[]{:S(2)}) async-start(), calls=%async_computation.1 | async-start | bytes 21221376 | tf_op jit(solution)/shard_map/all_gather | solution.py:16
  10.3 147.2 %copy-start = (f32[32,152]{1,0:T(8,128)S(1)}, f32[32,152]{1,0:T(8,128)}, u32[]{:S(2)}) copy-start(f32[32,152]{1,0:T(8,128)} %param.8) | copy-start | bytes 58372
  10.3 147.2 %reduce-scatter.2.cloned.1.call-start = ((), (), s32[]{:S(2)}) async-start(), calls=%async_computation.2 | async-start | bytes 294912 | tf_op jit(solution)/shard_map/reduce_scatter | solution.py:24
Sparse Core Ops, SparseCore 0:
  10.4 89.4 all-gather.1
  121.2 36.2 reduce-scatter.1
where the time goes:
time: 166 us
  waiting for transfers between devices  126 us (76%)
  matrix products  21.2 us (13%)
  between operations  13.4 us (8%)
  other arithmetic  4.19 us (3%)
    all_gather x1, waiting for transfers between devices, body(): whole = lax.all_gather(allowed, 'rows', axis=0, tiled=True)  89.6 us
    reduce_scatter x1, waiting for transfers between devices, body(): ladder = lax.psum_scatter(terms, 'blk', scatter_dimension=0, tiled=True)  36.4 us
    dot_general x1, matrix products, body(): lax.dot_general(whole, ladder_ints, (((1,), (1,)), ((), ())), precision=l...  21.2 us
  transfers between devices with their start and end apart: 2, of which 2 were waited for; matrix products, arithmetic and copies ran while one was open for 0% of the time, Pallas kernels for 0%

commit v1 on v0

v1 whole, which is shorter than its diff:
```python
import functools

import jax
import jax.numpy as jnp
from jax import lax
from jax.experimental import pallas as pl
from jax.experimental.pallas import tpu as pltpu
from jax.sharding import PartitionSpec as P

BF = jnp.bfloat16
F32 = jnp.float32
I32 = jnp.int32

NV = 400
NI = 8
PER = 50
CN = 50
WIN = 512
OJ = 8
OP = 256
ABD = 152
ABP = 160
PAY = 2560
GRP = 10
LW = 2048
CD = CN * NV
HOPS = (0, 2, 1, 3)
VMEM_LIMIT = 56 * 1024 * 1024


def nt(a, b):
    return lax.dot_general(a, b, (((1,), (1,)), ((), ())), preferred_element_type=F32)


def split(x):
    hi = x.astype(BF)
    return hi, (x - hi.astype(F32)).astype(BF)


def where_in_lanes(lane, pieces):
    out = pieces[-1][1]
    for edge, x in reversed(pieces[:-1]):
        out = jnp.where(lane < edge, x, out)
    return out


def compact_kernel(blk, virt_s, pair_s, virt_v, amp, pay, aux):
    c0 = blk() * CN
    lane = lax.broadcasted_iota(I32, (8, WIN), 1)
    sub = lax.broadcasted_iota(I32, (8, WIN), 0)
    irrep = jnp.concatenate([virt_v[...], jnp.full((1, WIN - NV), -1, I32)], axis=1)
    irrep = jnp.broadcast_to(irrep, (8, WIN))
    member = irrep == sub
    before = lax.broadcasted_iota(I32, (WIN, WIN), 0) < lax.broadcasted_iota(I32, (WIN, WIN), 1)
    count = jnp.dot(
        jnp.where(member, 1.0, 0.0).astype(BF),
        jnp.where(before, 1.0, 0.0).astype(BF),
        preferred_element_type=F32,
    )
    rank = jnp.sum(jnp.where(member, count, 0.0), axis=0, keepdims=True).astype(I32)
    rank = jnp.where(lane < NV, jnp.broadcast_to(rank, (8, WIN)), -1)
    aux[0:8, :] = rank
    aux[8:16, :] = irrep
    pair = jnp.zeros((8, WIN), I32)
    for i in range(OJ):
        pair = jnp.where(sub == i, pair_s[i], pair)
    need = jnp.where(lane < NV, jnp.bitwise_xor(irrep, pair), -1)
    row = lax.broadcasted_iota(I32, (128, WIN), 0)
    rows = {}
    for v in range(8):
        need_v = pltpu.roll(need, 16 * v, 1) if v else need
        rank_v = pltpu.roll(rank, 16 * v, 1) if v else rank
        pick = jnp.where(jnp.broadcast_to(rank_v[0:1, :], (128, WIN)) == row, 1.0, 0.0).astype(BF)
        cs = list(range(v, CN, 8))
        xs = []
        for c in cs:
            first = (NV * c) // 128 * 128
            width = min(WIN, CD - first)
            x = amp[:, first : first + width]
            if width < WIN:
                x = jnp.concatenate([x, jnp.zeros((8, WIN - width), F32)], axis=1)
            xs.append(jnp.where(need_v == virt_s[c0 + c], x, 0.0))
        if len(xs) % 2:
            xs.append(jnp.zeros((8, WIN), F32))
        hi, lo = split(jnp.concatenate(xs, axis=0))
        r = nt(hi, pick) + nt(lo, pick)
        for i, c in enumerate(cs):
            rows[c] = r[8 * i : 8 * i + 8, :]
    lane = lax.broadcasted_iota(I32, (8, 128), 1)
    for q in range(GRP):
        r0, r1, r2, r3, r4 = (rows[5 * q + e] for e in range(5))
        r1 = pltpu.roll(r1, 50, 1)
        r2a = pltpu.roll(r2, 100, 1)
        r2b = pltpu.roll(r2, 103, 1)
        r3 = pltpu.roll(r3, 25, 1)
        r4 = pltpu.roll(r4, 75, 1)
        a = where_in_lanes(lane, [(50, r0), (100, r1), (125, r2a), (128, jnp.zeros_like(r0))])
        b = where_in_lanes(lane, [(25, r2b), (75, r3), (128, r4)])
        if q == GRP - 1:
            b = jnp.where(lane == 127, pair[:, 0:128].astype(F32), b)
        pay[:, 256 * q : 256 * q + 128] = a
        pay[:, 256 * q + 128 : 256 * q + 256] = b


def sort_kernel(blk, q0, nq, virt_s, aux, tail, main, lhi, llo, b, m):
    g = pl.program_id(0)
    q = g + q0
    c0 = blk() * CN

    b[ABD - 8 : ABP, :] = jnp.zeros((ABP - ABD + 8, 2560), BF)
    b[ABP + ABD - 8 : 2 * ABP, :] = jnp.zeros((ABP - ABD + 8, 2560), BF)
    for first, width, src in ((0, 512, tail), (512, LW, main)):
        x = src[...]
        if q0 + nq == GRP and src is main:
            at = lax.broadcasted_iota(I32, (ABD, width), 1) + LW * q
            x = jnp.where(at < CD, x, 0.0)
        hi, lo = split(x)
        b[0:ABD, first : first + width] = hi
        b[ABP : ABP + ABD, first : first + width] = lo
    row = lax.broadcasted_iota(I32, (128, WIN), 0)
    parts = []
    for e in range(5):
        start = 512 + NV * e - 48 * q
        first = pl.multiple_of(start // 128 * 128, 128)
        shift = start - first
        rank = pltpu.roll(aux[0:8, :], shift, 1)
        irrep = pltpu.roll(aux[8:16, :], shift, 1)
        inside = rank >= 0
        sector = jnp.bitwise_xor(irrep, virt_s[c0 + 5 * q + e])
        place = rank + 50 * e
        place = jnp.where(place >= 125, place - 125, place)
        place = jnp.bitwise_and(place + 64 * jnp.bitwise_and(sector, 1), 127)
        place = jnp.where(inside, place, -1)
        pick = jnp.where(jnp.broadcast_to(place[0:1, :], (128, WIN)) == row, 1.0, 0.0).astype(BF)
        half = jnp.where(inside, lax.shift_right_logical(sector, 1), -1)
        for u in range(4):
            on = jnp.where(half[0:1, :] == u, 1.0, 0.0).astype(BF)
            m[128 * u : 128 * u + 128, :] = pick * jnp.broadcast_to(on, (128, WIN))
        parts.append(nt(b[:, pl.ds(first, WIN)], m[...]))
    lane = lax.broadcasted_iota(I32, (2 * ABP, 128), 1)
    turned = jnp.bitwise_and(lane + 64, 127)
    for u in range(4):
        r = [p[:, 128 * u : 128 * u + 128] for p in parts]
        for odd in range(2):
            at = turned if odd else lane
            for t in range(2):
                edges = [(50, r[0]), (100, r[1]), (128, r[2])] if t == 0 else [(25, r[2]), (75, r[3]), (128, r[4])]
                x = where_in_lanes(at, edges)
                if odd:
                    x = pltpu.roll(x, 64, 1)
                x = x.astype(BF)
                lhi[2 * u + odd, :, 128 * t : 128 * t + 128] = x[0:ABP]
                llo[2 * u + odd, :, 128 * t : 128 * t + 128] = x[ABP : 2 * ABP]


def main_kernel(rows, widths, *refs):
    n = len(widths)
    pieces = refs[:8]
    ls = refs[8 : 8 + 2 * n]
    out, gath, ghi, glo, acc, pair, sems = refs[8 + 2 * n :]
    s = pl.program_id(0)

    @pl.when(s == 0)
    def _():
        me = rows()
        core, y, x = me % 2, (me // 2) % 4, me // 8
        copies = []
        for j in range(8):
            far = j // 4
            kind = jnp.where(far == 1, 1 - core, core)
            d2 = HOPS[j % 4]
            for i in range(4):
                d1 = HOPS[i]
                dx = jnp.where(kind == 0, d1, d2)
                dy = jnp.where(kind == 0, d2, d1)
                xx = (x + 4 - dx) % 4
                yy = (y + 4 - dy) % 4
                shard = (xx * 4 + yy) * 2 + kind
                at = pl.multiple_of(shard * OJ, OJ)
                copies.append(
                    pltpu.make_async_copy(pieces[j].at[pl.ds(8 * i, 8), :], gath.at[pl.ds(at, OJ), :], sems.at[j, i])
                )
        for c in copies:
            c.start()
        for c in copies:
            c.wait()
        for k in range(0, PAY, 512):
            hi, lo = split(gath[:, k : k + 512])
            ghi[:, k : k + 512] = hi
            glo[:, k : k + 512] = lo
        last = gath[:, PAY - 128 : PAY]
        pair[...] = jnp.transpose(last)[120:128, :]
        acc[...] = jnp.zeros_like(acc)

    total = jnp.zeros((ABP, OP), F32)
    k = 0
    for i, w in enumerate(widths):
        hi = ls[2 * i][0]
        lo = ls[2 * i + 1][0]
        total = total + nt(hi, ghi[:, k : k + w])
        total = total + nt(lo, ghi[:, k : k + w])
        total = total + nt(hi, glo[:, k : k + w])
        k += w
    mine = jnp.broadcast_to(pair[7:8, :], (ABP, OP)) == s.astype(F32)
    acc[...] += jnp.where(mine, total, 0.0)

    @pl.when(s == NI - 1)
    def _():
        out[...] = jnp.transpose(acc[...])[:, 0:ABD]


def smem():
    return pl.BlockSpec(memory_space=pltpu.SMEM)


def compact(blk, virt, pair, amp):
    vmem = pl.BlockSpec(memory_space=pltpu.VMEM)
    return pl.pallas_call(
        functools.partial(compact_kernel, blk),
        out_shape=(jax.ShapeDtypeStruct((OJ, PAY), F32), jax.ShapeDtypeStruct((16, WIN), I32)),
        in_specs=[smem(), smem(), vmem, vmem],
        out_specs=(vmem, vmem),
        compiler_params=pltpu.CompilerParams(vmem_limit_bytes=VMEM_LIMIT),
        name="compact",
    )(virt, pair, virt.reshape(1, NV), amp)


def sort_part(blk, q0, nq, virt, aux, ints):
    shape = jax.ShapeDtypeStruct((NI, ABP, 256 * nq), BF)
    return pl.pallas_call(
        functools.partial(sort_kernel, blk, q0, nq),
        out_shape=(shape, shape),
        grid=(nq,),
        in_specs=[
            smem(),
            pl.BlockSpec((16, WIN), lambda g: (0, 0)),
            pl.BlockSpec((ABD, 512), lambda g: (0, jnp.maximum(4 * (g + q0) - 1, 0))),
            pl.BlockSpec((ABD, LW), lambda g: (0, g + q0)),
        ],
        out_specs=(
            pl.BlockSpec((NI, ABP, 256), lambda g: (0, 0, g)),
            pl.BlockSpec((NI, ABP, 256), lambda g: (0, 0, g)),
        ),
        scratch_shapes=[pltpu.VMEM((2 * ABP, 2560), BF), pltpu.VMEM((512, WIN), BF)],
        compiler_params=pltpu.CompilerParams(vmem_limit_bytes=VMEM_LIMIT),
        cost_estimate=pl.CostEstimate(flops=nq * 5 * 2 * 320 * 512 * 512, bytes_accessed=nq * 3000000, transcendentals=0),
        name="sort_ints",
    )(virt, aux, ints, ints)


def contract(rows, pieces, parts):
    widths = tuple(p[0].shape[2] for p in parts)
    flat = [x for p in parts for x in p]
    return pl.pallas_call(
        functools.partial(main_kernel, rows, widths),
        out_shape=jax.ShapeDtypeStruct((OP, ABD), F32),
        grid=(NI,),
        in_specs=[pl.BlockSpec(memory_space=pl.ANY)] * 8
        + [pl.BlockSpec((1, ABP, x.shape[2]), lambda s: (s, 0, 0)) for x in flat],
        out_specs=pl.BlockSpec((OP, ABD), lambda s: (0, 0)),
        scratch_shapes=[
            pltpu.VMEM((OP, PAY), F32),
            pltpu.VMEM((OP, PAY), BF),
            pltpu.VMEM((OP, PAY), BF),
            pltpu.VMEM((ABP, OP), F32),
            pltpu.VMEM((8, OP), F32),
            pltpu.SemaphoreType.DMA((8, 4)),
        ],
        compiler_params=pltpu.CompilerParams(vmem_limit_bytes=VMEM_LIMIT),
        cost_estimate=pl.CostEstimate(flops=3 * 2 * 1280 * 2560 * 256, bytes_accessed=16000000, transcendentals=0),
        name="contract",
    )(*pieces, *flat)


def at(x, y, core):
    return ((x % 4) * 4 + y % 4) * 2 + core


def walk(hop, second):
    pairs = []
    for x in range(4):
        for y in range(4):
            for core in range(2):
                along_x = (core == 0) != second
                to = at(x + hop, y, core) if along_x else at(x, y + hop, core)
                pairs.append((at(x, y, core), to))
    return pairs


SWAP = [(i, i ^ 1) for i in range(32)]


def body(amplitudes, pair_irrep, virt_irrep, resid_in, ladder_ints):
    blk = functools.partial(lax.axis_index, "blk")
    rows = functools.partial(lax.axis_index, "rows")
    pay, aux = compact(blk, virt_irrep, pair_irrep, amplitudes)
    first = [pay] + [lax.ppermute(pay, "rows", walk(h, False)) for h in HOPS[1:]]
    parts = [sort_part(blk, 0, 3, virt_irrep, aux, ladder_ints)]
    four = jnp.concatenate(first, axis=0)
    near = [four] + [lax.ppermute(four, "rows", walk(h, True)) for h in HOPS[1:]]
    parts.append(sort_part(blk, 3, 4, virt_irrep, aux, ladder_ints))
    far = [lax.ppermute(p, "rows", SWAP) for p in near]
    parts.append(sort_part(blk, 7, 3, virt_irrep, aux, ladder_ints))
    terms = contract(rows, near + far, parts)
    got = lax.all_to_all(terms.reshape(8, 32, ABD), "blk", 0, 0)
    return resid_in + jnp.sum(got, axis=0)


def solution(mesh):
    placed = (P("rows", "blk"), P("rows"), P(), P("blk", "rows"), P("rows", "blk"))
    return jax.shard_map(
        body, mesh=mesh, in_specs=placed, out_specs=P("blk", "rows"), check_vma=False
    )
```

time: 166 us -> 85.9 us (0.52)
  waiting for transfers between devices: 126 us -> 5.35 us
  Pallas kernels: 0 us -> 45 us
  matrix products: 21.2 us -> 0 us
  blocking collectives: 0 us -> 20.8 us
  between operations: 13.4 us -> 0.17 us
  starting transfers between devices: 0.04 us -> 10.5 us
  other arithmetic: 4.19 us -> 0.64 us
    all_gather x1 -> x0, waiting for transfers between devices: 89.6 us -> none  [body(): whole = lax.all_gather(allowed, 'rows', axis=0, tiled=True)]
    pallas_call x0 -> x5, Pallas kernels: none -> 45 us  [the longest x3 25.6 us: sort_part(): pl.pallas_call(functools.partial(sort_kernel, blk, q0, nq), out_shape=(sh...]
    reduce_scatter x1 -> x0, waiting for transfers between devices: 36.4 us -> none  [body(): ladder = lax.psum_scatter(terms, 'blk', scatter_dimension=0, tiled=True)]
    dot_general x1 -> x0, matrix products: 21.2 us -> none  [body(): lax.dot_general(whole, ladder_ints, (((1,), (1,)), ((), ())), precision=l...]
    all_to_all x0 -> x1, blocking collectives: none -> 20.8 us  [body(): got = lax.all_to_all(terms.reshape(8, 32, ABD), 'blk', 0, 0)]
    ppermute x0 -> x10, starting transfers between devices: none -> 10.5 us  [the longest x3 5.81 us: body(): lax.ppermute(four, 'rows', walk(h, True))]
    ppermute x0 -> x10, waiting for transfers between devices: none -> 5.35 us  [the longest x3 4.79 us: body(): lax.ppermute(pay, 'rows', walk(h, False))]
    select_n x1 -> x0, other arithmetic: 2.06 us -> none  [body(): jnp.where(sector[None, :] == pair_irrep[:, None], amplitudes, jnp.zeros_l...]
  transfers between devices with their start and end apart: 2 -> 10, of which waited for: 2 -> 2; matrix products, arithmetic and copies ran while one was open for 0% -> 1% of each run, Pallas kernels for 0% -> 30%
where the time goes in v1:
time: 85.9 us; the launch traced here: 84.5 us
  Pallas kernels  45 us (52%)
  blocking collectives  20.8 us (24%)
  starting transfers between devices  10.5 us (12%)
  waiting for transfers between devices  5.35 us (6%)
  local copies, waits for them, and re-layouts  1.97 us (2%)
    pallas_call x3, Pallas kernels, sort_part(): pl.pallas_call(functools.partial(sort_kernel, blk, q0, nq), out_shape=(sh...  25.6 us
    all_to_all x1, blocking collectives, body(): got = lax.all_to_all(terms.reshape(8, 32, ABD), 'blk', 0, 0)  20.8 us
    pallas_call x1, Pallas kernels, contract(): pl.pallas_call(functools.partial(main_kernel, rows, widths), out_shape=ja...  16.5 us
    ppermute x3, starting transfers between devices, body(): lax.ppermute(four, 'rows', walk(h, True))  5.81 us
    ppermute x3, waiting for transfers between devices, body(): lax.ppermute(pay, 'rows', walk(h, False))  4.79 us
    ppermute x3, starting transfers between devices, body(): lax.ppermute(pay, 'rows', walk(h, False))  3.68 us
    pallas_call x1, Pallas kernels, compact(): pl.pallas_call(functools.partial(compact_kernel, blk), out_shape=(jax.Sha...  2.87 us
    unnamed x21, local copies, waits for them, and re-layouts  1.97 us
  transfers between devices with their start and end apart: 10, of which 2 were waited for; matrix products, arithmetic and copies ran while one was open for 1% of the time, Pallas kernels for 30%

profile of v1, /device:TPU:6, one launch (start us, length us, event | category | flops | bytes accessed | tf_op | source)
XLA Modules:
  0.0 84.5 jit_solution(8446109352834912963)
XLA Ops:
  0.0 2.9 %compact.1 = (f32[8,2560]{1,0:T(8,128)}, s32[16,512]{1,0:T(8,128)}) custom-call(s32[400]{0:T(512)} %virt_s.7, s32[8]{0:T(128)} %pair_s.1, s32[1,400]{1,0:T(1,128)} %bitcast.3, f32[8,20000]{1,0:T(8,128)} %amp.1), custom_call_target="tpu_custom_call" | custom-call | tf_op jit(solution)/shard_map/compact/pallas_call | solution.py:218
  2.9 0.8 collective-permute-start.2
  3.7 2.4 %collective-permute-start.1 = (f32[8,2560]{1,0:T(8,128)}, f32[8,2560]{1,0:T(8,128)S(1)}, u32[]{:S(2)}, u32[]{:S(2)}) collective-permute-start(f32[8,2560]{1,0:T(8,128)} %get-tuple-element.13), channel_id=1, source_target_pairs={{0,64},{8,24},{16,80},{24,40},{32,96},{40,56},{48,112},{56,8},{64,... | collective-permute-start | bytes 245768 | tf_op jit(solution)/shard_map/ppermute | solution.py:297
  6.1 0.4 collective-permute-start
  6.6 0.9 %constant_dynamic-update-slice_fusion.3 = f32[32,2560]{1,0:T(8,128)S(1)} fusion(f32[8,2560]{1,0:T(8,128)} %get-tuple-element.13), kind=kLoop, calls=%fused_computation.3 | loop fusion | bytes 163840
  7.5 4.8 %collective-permute-done = f32[8,2560]{1,0:T(8,128)S(1)} collective-permute-done((f32[8,2560]{1,0:T(8,128)}, f32[8,2560]{1,0:T(8,128)S(1)}, u32[]{:S(2)}, u32[]{:S(2)}) %collective-permute-start) | collective-permute-done | bytes 81952 | tf_op jit(solution)/shard_map/ppermute | solution.py:297
  12.3 0.0 collective-permute-done.1
  12.3 0.0 collective-permute-done.2
  12.3 3.1 %collective-permute-start.5 = (f32[32,2560]{1,0:T(8,128)S(1)}, f32[32,2560]{1,0:T(8,128)S(1)}, u32[]{:S(2)}, u32[]{:S(2)}) collective-permute-start(f32[32,2560]{1,0:T(8,128)S(1)} %constant_dynamic-update-slice_fusion.refs_0_), channel_id=1, source_target_pairs={{0,48},{8,200},{16,0},{24,216},{32,16},{40,232},{48,32},{56,248},{... | collective-permute-start | bytes 983048 | tf_op jit(solution)/shard_map/ppermute | solution.py:300
  15.4 0.0 collective-permute-start.4
  15.4 2.7 %collective-permute-start.3 = (f32[32,2560]{1,0:T(8,128)S(1)}, f32[32,2560]{1,0:T(8,128)S(1)}, u32[]{:S(2)}, u32[]{:S(2)}) collective-permute-start(f32[32,2560]{1,0:T(8,128)S(1)} %constant_dynamic-update-slice_fusion.refs_0_), channel_id=1, source_target_pairs={{0,32},{8,136},{16,48},{24,152},{32,0},{40,168},{48,16},{56,184},{... | collective-permute-start | bytes 983048 | tf_op jit(solution)/shard_map/ppermute | solution.py:300
  18.1 8.0 %sort_ints.5 = (bf16[8,160,768]{2,1,0:T(8,128)(2,1)}, bf16[8,160,768]{2,1,0:T(8,128)(2,1)}) custom-call(s32[400]{0:T(512)} %virt_s.7, s32[16,512]{1,0:T(8,128)} %get-tuple-element.14.aux, f32[152,20000]{1,0:T(8,128)} %main.5, f32[152,20000]{1,0:T(8,128)} %main.5), custom_call_target="tpu_custom_call" | custom-call | flops 2516582400 | bytes 9000000 | tf_op jit(solution)/shard_map/sort_ints/pallas_call | solution.py:230
  26.2 0.0 collective-permute-start.6
  26.2 0.0 collective-permute-done.5.refs_3_
  26.2 0.5 collective-permute-start.9
  26.7 0.5 collective-permute-done.4.refs_2_
  27.2 0.0 collective-permute-start.8
  27.2 0.0 collective-permute-done.3.refs_1_
  27.2 0.5 collective-permute-start.7
  27.7 7.9 %sort_ints.3 = (bf16[8,160,768]{2,1,0:T(8,128)(2,1)}, bf16[8,160,768]{2,1,0:T(8,128)(2,1)}) custom-call(s32[400]{0:T(512)} %virt_s.7, s32[16,512]{1,0:T(8,128)} %get-tuple-element.14.aux, f32[152,20000]{1,0:T(8,128)} %main.5, f32[152,20000]{1,0:T(8,128)} %main.5), custom_call_target="tpu_custom_call" | custom-call | flops 2516582400 | bytes 9000000 | tf_op jit(solution)/shard_map/sort_ints/pallas_call | solution.py:230
  35.7 9.7 %sort_ints.4 = (bf16[8,160,1024]{2,1,0:T(8,128)(2,1)}, bf16[8,160,1024]{2,1,0:T(8,128)(2,1)}) custom-call(s32[400]{0:T(512)} %virt_s.7, s32[16,512]{1,0:T(8,128)} %get-tuple-element.14.aux, f32[152,20000]{1,0:T(8,128)} %main.5, f32[152,20000]{1,0:T(8,128)} %main.5), custom_call_target="tpu_custom_call" | custom-call | flops 3355443200 | bytes 12000000 | tf_op jit(solution)/shard_map/sort_ints/pallas_call | solution.py:230
  45.4 0.0 collective-permute-done.6.refs_4_
  45.4 0.0 collective-permute-done.9.refs_7_
  45.4 0.0 collective-permute-done.8.refs_6_
  45.4 0.0 collective-permute-done.7.refs_5_
  45.5 0.7 copy-done.5
  46.1 0.1 copy-done.6
  46.2 0.1 copy-done.7
  46.4 0.1 copy-done.8
  46.5 16.5 %contract.1 = f32[256,152]{1,0:T(8,128)} custom-call(f32[32,2560]{1,0:T(8,128)} %copy-done.1, f32[32,2560]{1,0:T(8,128)} %copy-done.4, f32[32,2560]{1,0:T(8,128)} %copy-done.3, f32[32,2560]{1,0:T(8,128)} %copy-done.2, f32[32,2560]{1,0:T(8,128)} %copy-done.5, f32[32,2560]{1,0:T(8,128)} %copy-done.8, f32[32,2560]{1,0:T(8,128)} %copy-done.7, ...), custom_call_target="tpu_custom_call" | custom-call | flops 5033164800 | bytes 16000000 | tf_op jit(solution)/shard_map/contract/pallas_call | solution.py:254
  63.0 20.8 %all_to_all.5 = f32[8,32,152]{2,1,0:T(8,128)S(1)} all-to-all(f32[8,32,152]{2,1,0:T(8,128)} %bitcast.2), channel_id=1, replica_groups=mesh['rows'=32,'blk'=8] {'blk'}, dimensions={0} | all-to-all | bytes 311296 | tf_op jit(solution)/shard_map/all_to_all | solution.py:305
  83.8 0.6 add.3
  (18 shorter events, 0.1 us)
Async XLA Ops:
  2.9 9.4 %collective-permute-start.2 = (f32[8,2560]{1,0:T(8,128)}, f32[8,2560]{1,0:T(8,128)S(1)}, u32[]{:S(2)}, u32[]{:S(2)}) collective-permute-start(f32[8,2560]{1,0:T(8,128)} %get-tuple-element.13), channel_id=1, source_target_pairs={{0,192},{8,56},{16,208},{24,8},{32,224},{40,24},{48,240},{56,40},{... | collective-permute-start | bytes 245768 | tf_op jit(solution)/shard_map/ppermute | solution.py:297
  3.7 8.6 %collective-permute-start.1 = (f32[8,2560]{1,0:T(8,128)}, f32[8,2560]{1,0:T(8,128)S(1)}, u32[]{:S(2)}, u32[]{:S(2)}) collective-permute-start(f32[8,2560]{1,0:T(8,128)} %get-tuple-element.13), channel_id=1, source_target_pairs={{0,64},{8,24},{16,80},{24,40},{32,96},{40,56},{48,112},{56,8},{64,... | collective-permute-start | bytes 245768 | tf_op jit(solution)/shard_map/ppermute | solution.py:297
  6.1 6.2 %collective-permute-start = (f32[8,2560]{1,0:T(8,128)}, f32[8,2560]{1,0:T(8,128)S(1)}, u32[]{:S(2)}, u32[]{:S(2)}) collective-permute-start(f32[8,2560]{1,0:T(8,128)} %get-tuple-element.13), channel_id=1, source_target_pairs={{0,128},{8,40},{16,144},{24,56},{32,160},{40,8},{48,176},{56,24},{... | collective-permute-start | bytes 245768 | tf_op jit(solution)/shard_map/ppermute | solution.py:297
  12.3 13.8 %copy-start.1 = (f32[32,2560]{1,0:T(8,128)}, f32[32,2560]{1,0:T(8,128)S(1)}, u32[]{:S(2)}) copy-start(f32[32,2560]{1,0:T(8,128)S(1)} %constant_dynamic-update-slice_fusion.refs_0_) | copy-start | bytes 983044
  12.3 13.8 %collective-permute-start.5 = (f32[32,2560]{1,0:T(8,128)S(1)}, f32[32,2560]{1,0:T(8,128)S(1)}, u32[]{:S(2)}, u32[]{:S(2)}) collective-permute-start(f32[32,2560]{1,0:T(8,128)S(1)} %constant_dynamic-update-slice_fusion.refs_0_), channel_id=1, source_target_pairs={{0,48},{8,200},{16,0},{24,216},{32,16},{40,232},{48,32},{56,248},{... | collective-permute-start | bytes 983048 | tf_op jit(solution)/shard_map/ppermute | solution.py:300
  15.4 11.8 %collective-permute-start.4 = (f32[32,2560]{1,0:T(8,128)S(1)}, f32[32,2560]{1,0:T(8,128)S(1)}, u32[]{:S(2)}, u32[]{:S(2)}) collective-permute-start(f32[32,2560]{1,0:T(8,128)S(1)} %constant_dynamic-update-slice_fusion.refs_0_), channel_id=1, source_target_pairs={{0,16},{8,72},{16,32},{24,88},{32,48},{40,104},{48,0},{56,120},{64... | collective-permute-start | bytes 983048 | tf_op jit(solution)/shard_map/ppermute | solution.py:300
  15.4 11.8 %collective-permute-start.3 = (f32[32,2560]{1,0:T(8,128)S(1)}, f32[32,2560]{1,0:T(8,128)S(1)}, u32[]{:S(2)}, u32[]{:S(2)}) collective-permute-start(f32[32,2560]{1,0:T(8,128)S(1)} %constant_dynamic-update-slice_fusion.refs_0_), channel_id=1, source_target_pairs={{0,32},{8,136},{16,48},{24,152},{32,0},{40,168},{48,16},{56,184},{... | collective-permute-start | bytes 983048 | tf_op jit(solution)/shard_map/ppermute | solution.py:300
  26.2 19.2 %collective-permute-start.6 = (f32[32,2560]{1,0:T(8,128)S(1)}, f32[32,2560]{1,0:T(8,128)S(1)}, u32[]{:S(2)}, u32[]{:S(2)}) collective-permute-start(f32[32,2560]{1,0:T(8,128)S(1)} %constant_dynamic-update-slice_fusion.refs_0_), channel_id=1, source_target_pairs={{0,8},{8,0},{16,24},{24,16},{32,40},{40,32},{48,56},{56,48},{64,72... | collective-permute-start | bytes 983048 | tf_op jit(solution)/shard_map/ppermute | solution.py:302
  26.2 9.5 %copy-start.2 = (f32[32,2560]{1,0:T(8,128)}, f32[32,2560]{1,0:T(8,128)S(1)}, u32[]{:S(2)}) copy-start(f32[32,2560]{1,0:T(8,128)S(1)} %collective-permute-done.5.refs_3_) | copy-start | bytes 983044
  26.2 19.2 %collective-permute-start.9 = (f32[32,2560]{1,0:T(8,128)S(1)}, f32[32,2560]{1,0:T(8,128)S(1)}, u32[]{:S(2)}, u32[]{:S(2)}) collective-permute-start(f32[32,2560]{1,0:T(8,128)S(1)} %collective-permute-done.5.refs_3_), channel_id=1, source_target_pairs={{0,8},{8,0},{16,24},{24,16},{32,40},{40,32},{48,56},{56,48},{64,72... | collective-permute-start | bytes 983048 | tf_op jit(solution)/shard_map/ppermute | solution.py:302
  27.2 8.4 %copy-start.3 = (f32[32,2560]{1,0:T(8,128)}, f32[32,2560]{1,0:T(8,128)S(1)}, u32[]{:S(2)}) copy-start(f32[32,2560]{1,0:T(8,128)S(1)} %collective-permute-done.4.refs_2_) | copy-start | bytes 983044
  27.2 18.2 %collective-permute-start.8 = (f32[32,2560]{1,0:T(8,128)S(1)}, f32[32,2560]{1,0:T(8,128)S(1)}, u32[]{:S(2)}, u32[]{:S(2)}) collective-permute-start(f32[32,2560]{1,0:T(8,128)S(1)} %collective-permute-done.4.refs_2_), channel_id=1, source_target_pairs={{0,8},{8,0},{16,24},{24,16},{32,40},{40,32},{48,56},{56,48},{64,72... | collective-permute-start | bytes 983048 | tf_op jit(solution)/shard_map/ppermute | solution.py:302
  27.2 8.4 %copy-start.4 = (f32[32,2560]{1,0:T(8,128)}, f32[32,2560]{1,0:T(8,128)S(1)}, u32[]{:S(2)}) copy-start(f32[32,2560]{1,0:T(8,128)S(1)} %collective-permute-done.3.refs_1_) | copy-start | bytes 983044
  27.2 18.2 %collective-permute-start.7 = (f32[32,2560]{1,0:T(8,128)S(1)}, f32[32,2560]{1,0:T(8,128)S(1)}, u32[]{:S(2)}, u32[]{:S(2)}) collective-permute-start(f32[32,2560]{1,0:T(8,128)S(1)} %collective-permute-done.3.refs_1_), channel_id=1, source_target_pairs={{0,8},{8,0},{16,24},{24,16},{32,40},{40,32},{48,56},{56,48},{64,72... | collective-permute-start | bytes 983048 | tf_op jit(solution)/shard_map/ppermute | solution.py:302
  45.4 0.8 copy-start.5
  45.4 0.8 copy-start.6
  45.4 0.9 %copy-start.7 = (f32[32,2560]{1,0:T(8,128)}, f32[32,2560]{1,0:T(8,128)S(1)}, u32[]{:S(2)}) copy-start(f32[32,2560]{1,0:T(8,128)S(1)} %collective-permute-done.8.refs_6_) | copy-start | bytes 983044
  45.4 1.0 %copy-start.8 = (f32[32,2560]{1,0:T(8,128)}, f32[32,2560]{1,0:T(8,128)S(1)}, u32[]{:S(2)}) copy-start(f32[32,2560]{1,0:T(8,128)S(1)} %collective-permute-done.7.refs_5_) | copy-start | bytes 983044
  46.5 37.4 %copy-start = (f32[32,152]{1,0:T(8,128)S(1)}, f32[32,152]{1,0:T(8,128)}, u32[]{:S(2)}) copy-start(f32[32,152]{1,0:T(8,128)} %param.8) | copy-start | bytes 58372

commit v2 on v1

v2 whole, which is shorter than its diff:
```python
import functools

import jax
import jax.numpy as jnp
from jax import lax
from jax.experimental import pallas as pl
from jax.experimental.pallas import tpu as pltpu
from jax.sharding import PartitionSpec as P

BF = jnp.bfloat16
F32 = jnp.float32
I32 = jnp.int32

NV = 400
NI = 8
PER = 50
CN = 50
WIN = 512
OJ = 8
OP = 256
ABD = 152
ABP = 160
PAY = 2560
GRP = 10
GW = 2048
SPAN = 2176
CD = CN * NV
EDGE = CD // 128 * 128
CHIPS = 16
SECT = 4
VMEM_LIMIT = 24 * 1024 * 1024
SORT_VMEM = 34 * 1024 * 1024


def nt(a, b):
    return lax.dot_general(a, b, (((1,), (1,)), ((), ())), preferred_element_type=F32)


def split(x):
    hi = x.astype(BF)
    return hi, (x - hi.astype(F32)).astype(BF)


def where_in_lanes(lane, pieces):
    out = pieces[-1][1]
    for edge, x in reversed(pieces[:-1]):
        out = jnp.where(lane < edge, x, out)
    return out


def turn(lane, x):
    moved = jnp.where(lane < 62, pltpu.roll(x, 65, 1), pltpu.roll(x, 62, 1))
    return jnp.where(lane < 125, moved, 0.0)


def compact_kernel(blk, virt_s, pair_s, virt_v, amp, edge, pays, aux, tail, pay, sem):
    c0 = blk() * CN
    lane = lax.broadcasted_iota(I32, (8, WIN), 1)
    sub = lax.broadcasted_iota(I32, (8, WIN), 0)
    irrep = jnp.concatenate([virt_v[...], jnp.full((1, WIN - NV), -1, I32)], axis=1)
    irrep = jnp.broadcast_to(irrep, (8, WIN))
    member = irrep == sub
    before = lax.broadcasted_iota(I32, (WIN, WIN), 0) < lax.broadcasted_iota(I32, (WIN, WIN), 1)
    count = jnp.dot(
        jnp.where(member, 1.0, 0.0).astype(BF),
        jnp.where(before, 1.0, 0.0).astype(BF),
        preferred_element_type=F32,
    )
    rank = jnp.sum(jnp.where(member, count, 0.0), axis=0, keepdims=True).astype(I32)
    rank = jnp.where(lane < NV, jnp.broadcast_to(rank, (8, WIN)), -1)
    aux[0:8, :] = rank
    aux[8:16, :] = irrep
    tail[...] = jnp.where(lax.broadcasted_iota(I32, (ABD, 128), 1) < CD - EDGE, edge[...], 0.0)
    pair = jnp.zeros((8, WIN), I32)
    for i in range(OJ):
        pair = jnp.where(sub == i, pair_s[i], pair)
    need = jnp.where(lane < NV, jnp.bitwise_xor(irrep, pair), -1)
    row = lax.broadcasted_iota(I32, (128, WIN), 0)
    rows = {}
    for v in range(8):
        need_v = pltpu.roll(need, 16 * v, 1) if v else need
        rank_v = pltpu.roll(rank, 16 * v, 1) if v else rank
        pick = jnp.where(jnp.broadcast_to(rank_v[0:1, :], (128, WIN)) == row, 1.0, 0.0).astype(BF)
        cs = list(range(v, CN, 8))
        xs = []
        for c in cs:
            first = (NV * c) // 128 * 128
            width = min(WIN, CD - first)
            x = amp[:, first : first + width]
            if width < WIN:
                x = jnp.concatenate([x, jnp.zeros((8, WIN - width), F32)], axis=1)
            xs.append(jnp.where(need_v == virt_s[c0 + c], x, 0.0))
        if len(xs) % 2:
            xs.append(jnp.zeros((8, WIN), F32))
        hi, lo = split(jnp.concatenate(xs, axis=0))
        r = nt(hi, pick) + nt(lo, pick)
        for i, c in enumerate(cs):
            rows[c] = r[8 * i : 8 * i + 8, :]
    lane = lax.broadcasted_iota(I32, (8, 128), 1)
    odd = jnp.bitwise_and(pair[:, 0:128], 1) == 1
    for q in range(GRP):
        r0, r1, r2, r3, r4 = (rows[5 * q + e] for e in range(5))
        r1 = pltpu.roll(r1, 50, 1)
        r2a = pltpu.roll(r2, 100, 1)
        r2b = pltpu.roll(r2, 103, 1)
        r3 = pltpu.roll(r3, 25, 1)
        r4 = pltpu.roll(r4, 75, 1)
        a = where_in_lanes(lane, [(50, r0), (100, r1), (125, r2a), (128, jnp.zeros_like(r0))])
        b = where_in_lanes(lane, [(25, r2b), (75, r3), (128, r4)])
        a = jnp.where(odd, turn(lane, a), a)
        b = jnp.where(odd, turn(lane, b), b)
        if q == GRP - 1:
            b = jnp.where(lane == 127, pair[:, 0:128].astype(F32), b)
        pay[:, 256 * q : 256 * q + 128] = a
        pay[:, 256 * q + 128 : 256 * q + 256] = b
    copies = [pltpu.make_async_copy(pay, pays.at[j], sem.at[j]) for j in range(CHIPS)]
    for c in copies:
        c.start()
    for c in copies:
        c.wait()


def chunk(q0, nq, i):
    q = q0 + i
    first = GW * q + (128 if i else 0) if i else NV * 5 * q0 // 128 * 128
    last = min(GW * (q + 1) + 128, EDGE)
    return first, last - first


def sort_kernel(blk, q0, nq, virt_s, aux, tail, ints, lhi, llo, x, ba, bb, ma, mb, sems):
    c0 = blk() * CN
    base = chunk(q0, nq, 0)[0]
    copies = []
    for i in range(nq):
        first, width = chunk(q0, nq, i)
        copies.append(
            pltpu.make_async_copy(
                ints.at[:, pl.ds(first, width)], x.at[:, pl.ds(first - base, width)], sems.at[i]
            )
        )
    for c in copies[:4]:
        c.start()
    if q0 + nq == GRP:
        x[:, EDGE - base : EDGE - base + 128] = tail[...]
    for b in (ba, bb):
        b[ABD - 8 : ABP, :] = jnp.zeros((ABP - ABD + 8, SPAN), BF)
        b[ABP + ABD - 8 : 2 * ABP, :] = jnp.zeros((ABP - ABD + 8, SPAN), BF)
    row = lax.broadcasted_iota(I32, (128, WIN), 0)
    lane = lax.broadcasted_iota(I32, (2 * ABP, 128), 1)
    turned = jnp.where(lane < 62, lane + 63, lane - 62).astype(F32).astype(BF)
    lane = lane.astype(F32).astype(BF)

    def load(i, b):
        begin = pl.multiple_of(NV * 5 * (q0 + i) // 128 * 128 - base, 128)
        hi, lo = split(x[:, pl.ds(begin, SPAN)])
        b[0:ABD, :] = hi
        b[ABP : ABP + ABD, :] = lo

    def sort(i, e, b, m):
        start = NV * 5 * (q0 + i)
        at = start - start // 128 * 128 + NV * e
        first = pl.multiple_of(at // 128 * 128, 128)
        rank = pltpu.roll(aux[0:8, :], at - first, 1)
        irrep = pltpu.roll(aux[8:16, :], at - first, 1)
        inside = rank >= 0
        sector = jnp.bitwise_xor(irrep, virt_s[c0 + 5 * (q0 + i) + e])
        place = rank + 50 * e
        place = jnp.where(place >= 125, place - 125, place)
        place = place + 62 * jnp.bitwise_and(sector, 1)
        place = jnp.where(place >= 125, place - 125, place)
        place = jnp.where(inside, place, -1)
        pick = jnp.where(jnp.broadcast_to(place[0:1, :], (128, WIN)) == row, 1.0, 0.0).astype(BF)
        half = jnp.where(inside, lax.shift_right_logical(sector, 1), -1)
        for u in range(4):
            on = jnp.where(half[0:1, :] == u, 1.0, 0.0).astype(BF)
            m[e, 128 * u : 128 * u + 128, :] = pick * jnp.broadcast_to(on, (128, WIN))
        return nt(b[:, pl.ds(first, WIN)], m[e]).astype(BF)

    def merge(i, u, parts):
        to = pl.multiple_of(256 * i, 256)
        r = [p[:, 128 * u : 128 * u + 128] for p in parts]
        for odd in range(2):
            at = turned if odd else lane
            for t in range(2):
                edges = [(50, r[0]), (100, r[1]), (128, r[2])] if t == 0 else [(25, r[2]), (75, r[3]), (128, r[4])]
                y = where_in_lanes(at, edges)
                lhi[2 * u + odd, :, pl.ds(to + 128 * t, 128)] = y[0:ABP]
                llo[2 * u + odd, :, pl.ds(to + 128 * t, 128)] = y[ABP : 2 * ABP]

    def pair(k, carry):
        i = 2 * k
        for j, c in enumerate(copies):
            pl.when(k == j // 2)(c.wait)
            if j >= 4:
                pl.when(k == j // 2 - 2)(c.start)
        load(i, ba)
        load(i + 1, bb)
        pa = [sort(i, e, ba, ma) for e in range(5)]
        pb = []
        for e in range(5):
            pb.append(sort(i + 1, e, bb, mb))
            if e < 4:
                merge(i, e, pa)
        for u in range(4):
            merge(i + 1, u, pb)
        return carry

    lax.fori_loop(0, nq // 2, pair, 0)


def main_kernel(core, widths, near, far, *refs):
    n = len(widths)
    ls = refs[: 2 * n]
    out, gath, ghi, glo, acc, pair, sems = refs[2 * n :]
    mine = core()
    copies = [
        pltpu.make_async_copy(src, gath.at[pl.ds(pl.multiple_of(half * 128, 128), 128), :], sems.at[i])
        for i, (src, half) in enumerate(((near, mine), (far, 1 - mine)))
    ]
    for c in copies:
        c.start()
    for c in copies:
        c.wait()
    for k in range(0, PAY, 512):
        hi, lo = split(gath[:, k : k + 512])
        ghi[:, k : k + 512] = hi
        glo[:, k : k + 512] = lo
    pair[...] = jnp.transpose(gath[:, PAY - 128 : PAY])[120:128, :]
    acc[...] = jnp.zeros_like(acc)

    def quarter(step, carry):
        total = None
        k = 0
        for i, w in enumerate(widths):
            hi = ls[2 * i][pl.ds(SECT * step, SECT)].reshape(SECT * ABP, w)
            lo = ls[2 * i + 1][pl.ds(SECT * step, SECT)].reshape(SECT * ABP, w)
            x = nt(hi, ghi[:, k : k + w]) + nt(lo, ghi[:, k : k + w]) + nt(hi, glo[:, k : k + w])
            total = x if total is None else total + x
            k += w
        part = acc[...]
        for i in range(SECT):
            own = jnp.broadcast_to(pair[7:8, :], (ABP, OP)) == (SECT * step + i).astype(F32)
            part = part + jnp.where(own, total[ABP * i : ABP * i + ABP, :], 0.0)
        acc[...] = part
        return carry

    lax.fori_loop(0, NI // SECT, quarter, 0)
    t = jnp.transpose(acc[...])
    for j in range(16):
        for c in range(2):
            out[16 * j + 8 * c : 16 * j + 8 * c + 8, :] = t[128 * c + 8 * j : 128 * c + 8 * j + 8, 0:ABD]


def smem():
    return pl.BlockSpec(memory_space=pltpu.SMEM)


def whole(shape):
    return pl.BlockSpec(shape, lambda g: (0,) * len(shape))


def compact(blk, virt, pair, amp, ints):
    return pl.pallas_call(
        functools.partial(compact_kernel, blk),
        out_shape=(
            jax.ShapeDtypeStruct((CHIPS, OJ, PAY), F32),
            jax.ShapeDtypeStruct((16, WIN), I32),
            jax.ShapeDtypeStruct((ABD, 128), F32),
        ),
        grid=(1,),
        in_specs=[
            smem(),
            smem(),
            whole((1, NV)),
            whole((OJ, CD)),
            pl.BlockSpec((ABD, 128), lambda g: (0, EDGE // 128)),
        ],
        out_specs=(pl.BlockSpec(memory_space=pl.ANY), whole((16, WIN)), whole((ABD, 128))),
        scratch_shapes=[pltpu.VMEM((OJ, PAY), F32), pltpu.SemaphoreType.DMA((CHIPS,))],
        compiler_params=pltpu.CompilerParams(vmem_limit_bytes=VMEM_LIMIT),
        name="compact",
    )(virt, pair, virt.reshape(1, NV), amp, ints)


def sort_part(blk, q0, nq, virt, aux, tail, ints):
    shape = pltpu.VMEM((NI, ABP, 256 * nq), BF)
    vmem = pl.BlockSpec(memory_space=pltpu.VMEM)
    begin = chunk(q0, nq, 0)[0]
    end = NV * 5 * (q0 + nq - 1) // 128 * 128 + SPAN
    end = max(end, sum(chunk(q0, nq, nq - 1)))
    return pl.pallas_call(
        functools.partial(sort_kernel, blk, q0, nq),
        out_shape=(shape, shape),
        in_specs=[smem(), vmem, vmem, pl.BlockSpec(memory_space=pl.ANY)],
        out_specs=(vmem, vmem),
        scratch_shapes=[
            pltpu.VMEM((ABD, end - begin), F32),
            pltpu.VMEM((2 * ABP, SPAN), BF),
            pltpu.VMEM((2 * ABP, SPAN), BF),
            pltpu.VMEM((5, 512, WIN), BF),
            pltpu.VMEM((5, 512, WIN), BF),
            pltpu.SemaphoreType.DMA((nq,)),
        ],
        compiler_params=pltpu.CompilerParams(vmem_limit_bytes=SORT_VMEM),
        cost_estimate=pl.CostEstimate(flops=nq * 5 * 2 * 320 * 512 * 512, bytes_accessed=nq * 1300000, transcendentals=0),
        name="sort_ints",
    )(virt, aux, tail, ints)


def contract(core, near, far, parts):
    widths = tuple(p[0].shape[2] for p in parts)
    flat = [x for p in parts for x in p]
    vmem = pl.BlockSpec(memory_space=pltpu.VMEM)
    return pl.pallas_call(
        functools.partial(main_kernel, core, widths),
        out_shape=jax.ShapeDtypeStruct((OP, ABD), F32),
        in_specs=[pl.BlockSpec(memory_space=pl.ANY)] * 2 + [vmem] * len(flat),
        out_specs=vmem,
        scratch_shapes=[
            pltpu.VMEM((OP, PAY), F32),
            pltpu.VMEM((OP, PAY), BF),
            pltpu.VMEM((OP, PAY), BF),
            pltpu.VMEM((ABP, OP), F32),
            pltpu.VMEM((8, OP), F32),
            pltpu.SemaphoreType.DMA((2,)),
        ],
        compiler_params=pltpu.CompilerParams(vmem_limit_bytes=VMEM_LIMIT),
        cost_estimate=pl.CostEstimate(flops=3 * 2 * 1280 * 2560 * 256, bytes_accessed=16000000, transcendentals=0),
        name="contract",
    )(near, far, *[pltpu.with_memory_space_constraint(x, pltpu.VMEM) for x in flat])


SWAP = [(i, i ^ 1) for i in range(32)]
PLANE = [[2 * chip + core for chip in range(CHIPS)] for core in range(2)]


def body(amplitudes, pair_irrep, virt_irrep, resid_in, ladder_ints):
    blk = functools.partial(lax.axis_index, "blk")
    pays, aux, tail = compact(blk, virt_irrep, pair_irrep, amplitudes, ladder_ints)
    near = lax.all_to_all(pays, "rows", 0, 0, axis_index_groups=PLANE).reshape(CHIPS * OJ, PAY)
    parts = [sort_part(blk, 0, 8, virt_irrep, aux, tail, ladder_ints)]
    far = lax.ppermute(near, "rows", SWAP)
    parts.append(sort_part(blk, 8, 2, virt_irrep, aux, tail, ladder_ints))
    terms = contract(lambda: lax.axis_index("rows") % 2, near, far, parts)
    got = lax.all_to_all(terms.reshape(8, 32, ABD), "blk", 0, 0)
    return resid_in + jnp.sum(got, axis=0)


def solution(mesh):
    placed = (P("rows", "blk"), P("rows"), P(), P("blk", "rows"), P("rows", "blk"))
    return jax.shard_map(
        body, mesh=mesh, in_specs=placed, out_specs=P("blk", "rows"), check_vma=False
    )
```

time: 85.9 us -> 85.2 us (level)
  the two profiles are of different devices: /device:TPU:6 before, /device:TPU:1 now
where the time goes in v2:
time: 85.2 us; the launch traced here: 85 us
  blocking collectives  46.6 us (55%)
  Pallas kernels  28.9 us (34%)
  local copies, waits for them, and re-layouts  6.91 us (8%)
  starting transfers between devices  1.79 us (2%)
    all_to_all x1, blocking collectives, body(): lax.all_to_all(pays, 'rows', 0, 0, axis_index_groups=PLANE)  26.3 us
    all_to_all x1, blocking collectives, body(): got = lax.all_to_all(terms.reshape(8, 32, ABD), 'blk', 0, 0)  20.3 us
    pallas_call x2, Pallas kernels, sort_part(): pl.pallas_call(functools.partial(sort_kernel, blk, q0, nq), out_shape=(sh...  18.9 us
    unnamed x14, local copies, waits for them, and re-layouts  6.91 us
    pallas_call x1, Pallas kernels, contract(): pl.pallas_call(functools.partial(main_kernel, core, widths), out_shape=ja...  6.42 us
    pallas_call x1, Pallas kernels, compact(): pl.pallas_call(functools.partial(compact_kernel, blk), out_shape=(jax.Sha...  3.63 us
    ppermute x1, starting transfers between devices, body(): far = lax.ppermute(near, 'rows', SWAP)  1.79 us
  transfers between devices with their start and end apart: 1, of which 0 were waited for; matrix products, arithmetic and copies ran while one was open for 0% of the time, Pallas kernels for 22%

profile of v2, /device:TPU:1, one launch (start us, length us, event | category | flops | bytes accessed | tf_op | source)
XLA Modules:
  0.0 85.0 jit_solution(14972701208601103700)
XLA Ops:
  0.0 0.0 copy-start
  0.0 4.5 %copy-done = f32[152,20000]{1,0:T(8,128)S(1)} copy-done((f32[152,20000]{1,0:T(8,128)S(1)}, f32[152,20000]{1,0:T(8,128)}, u32[]{:S(2)}) %copy-start) | copy-done | bytes 12160024
  4.5 0.0 copy-start.2
  4.5 1.1 %copy-done.2 = f32[8,20000]{1,0:T(8,128)S(1)} copy-done((f32[8,20000]{1,0:T(8,128)S(1)}, f32[8,20000]{1,0:T(8,128)}, u32[]{:S(2)}) %copy-start.2) | copy-done | bytes 640024
  5.6 0.0 copy-start.3
  5.6 0.7 copy-done.3
  6.2 0.0 copy-start.5
  6.2 0.7 copy-done.5
  6.9 0.0 copy-start.1
  6.9 3.6 %compact.1 = (f32[16,8,2560]{2,1,0:T(8,128)S(1)}, s32[16,512]{1,0:T(8,128)S(1)}, f32[152,128]{1,0:T(8,128)S(1)}) custom-call(s32[400]{0:T(512)S(1)} %copy-done.3, s32[8]{0:T(128)S(1)} %copy-done.5, s32[1,400]{1,0:T(1,128)S(1)} %bitcast.6, f32[8,20000]{1,0:T(8,128)S(1)} %copy-done.2, f32[152,20000]{1,0:T(8,128)S(1)} %copy-done), custom_call_target="tpu_custom_call" | custom-call | tf_op jit(solution)/shard_map/compact/pallas_call | solution.py:263
  10.5 0.0 copy-start.4
  10.5 26.3 %all_to_all.10 = f32[16,8,2560]{2,1,0:T(8,128)S(1)} all-to-all(f32[16,8,2560]{2,1,0:T(8,128)S(1)} %get-tuple-element.12), channel_id=1, replica_groups={{0,16,32,48,64,80,96,112,128,144,160,176,192,208,224,240},{8,24,40,56,7..., dimensions={0} | all-to-all | bytes 2621440 | tf_op jit(solution)/shard_map/all_to_all | solution.py:340
  36.8 1.8 %collective-permute-start = (f32[128,2560]{1,0:T(8,128)S(1)}, f32[128,2560]{1,0:T(8,128)S(1)}, u32[]{:S(2)}, u32[]{:S(2)}) collective-permute-start(f32[128,2560]{1,0:T(8,128)S(1)} %bitcast.3), channel_id=1, source_target_pairs={{0,8},{8,0},{16,24},{24,16},{32,40},{40,32},{48,56},{56,48},{64,72... | collective-permute-start | bytes 3932168 | tf_op jit(solution)/shard_map/ppermute | solution.py:342
  38.6 0.0 copy-done.1
  38.6 0.0 copy-done.4
  38.6 3.1 %sort_ints.3 = (bf16[8,160,512]{2,1,0:T(8,128)(2,1)S(1)}, bf16[8,160,512]{2,1,0:T(8,128)(2,1)S(1)}) custom-call(s32[400]{0:T(512)S(1)} %copy-done.4, s32[16,512]{1,0:T(8,128)S(1)} %get-tuple-element.13.aux, f32[152,128]{1,0:T(8,128)S(1)} %get-tuple-element.14.tail, f32[152,20000]{1,0:T(8,128)S(1)} %copy-done.1), custom_call_target="tpu_custom_call" | custom-call | flops 1677721600 | bytes 2600000 | tf_op jit(solution)/shard_map/sort_ints/pallas_call | solution.py:291
  41.7 15.8 %sort_ints.2 = (bf16[8,160,2048]{2,1,0:T(8,128)(2,1)S(1)}, bf16[8,160,2048]{2,1,0:T(8,128)(2,1)S(1)}) custom-call(s32[400]{0:T(512)S(1)} %copy-done.4, s32[16,512]{1,0:T(8,128)S(1)} %get-tuple-element.13.aux, f32[152,128]{1,0:T(8,128)S(1)} %get-tuple-element.14.tail, f32[152,20000]{1,0:T(8,128)} %ints.3), custom_call_target="tpu_custom_call" | custom-call | flops 6710886400 | bytes 10400000 | tf_op jit(solution)/shard_map/sort_ints/pallas_call | solution.py:291
  57.5 0.0 collective-permute-done.far
  57.5 0.0 copy-start.6
  57.5 6.4 %contract.1 = f32[256,152]{1,0:T(8,128)S(1)} custom-call(f32[128,2560]{1,0:T(8,128)S(1)} %bitcast.4, f32[128,2560]{1,0:T(8,128)S(1)} %collective-permute-done.far, bf16[8,160,2048]{2,1,0:T(8,128)(2,1)S(1)} %get-tuple-element.15.refs_0_, bf16[8,160,2048]{2,1,0:T(8,128)(2,1)S(1)} %get-tuple-element.16.refs_1_, ...), custom_call_target="tpu_custom_call" | custom-call | flops 5033164800 | bytes 16000000 | tf_op jit(solution)/shard_map/contract/pallas_call | solution.py:314
  64.0 20.3 %all_to_all.11 = f32[8,32,152]{2,1,0:T(8,128)S(1)} all-to-all(f32[8,32,152]{2,1,0:T(8,128)S(1)} %bitcast.5), channel_id=1, replica_groups=mesh['rows'=32,'blk'=8] {'blk'}, dimensions={0} | all-to-all | bytes 311296 | tf_op jit(solution)/shard_map/all_to_all | solution.py:345
  84.3 0.0 copy-done.6
  84.3 0.6 add.3
  (1 shorter events, 0.0 us)
Async XLA Ops:
  0.0 4.5 %copy-start = (f32[152,20000]{1,0:T(8,128)S(1)}, f32[152,20000]{1,0:T(8,128)}, u32[]{:S(2)}) copy-start(f32[152,20000]{1,0:T(8,128)} %ints.3) | copy-start | bytes 36480004
  4.5 1.1 %copy-start.2 = (f32[8,20000]{1,0:T(8,128)S(1)}, f32[8,20000]{1,0:T(8,128)}, u32[]{:S(2)}) copy-start(f32[8,20000]{1,0:T(8,128)} %amp.1) | copy-start | bytes 1920004
  5.6 0.7 copy-start.3
  6.2 0.7 copy-start.5
  6.9 31.7 %copy-start.1 = (f32[152,20000]{1,0:T(8,128)S(1)}, f32[152,20000]{1,0:T(8,128)}, u32[]{:S(2)}) copy-start(f32[152,20000]{1,0:T(8,128)} %ints.3) | copy-start | bytes 36480004
  10.5 28.1 %copy-start.4 = (s32[400]{0:T(512)S(1)}, s32[400]{0:T(512)}, u32[]{:S(2)}) copy-start(s32[400]{0:T(512)} %virt_s.5) | copy-start | bytes 4804
  36.8 20.7 %collective-permute-start = (f32[128,2560]{1,0:T(8,128)S(1)}, f32[128,2560]{1,0:T(8,128)S(1)}, u32[]{:S(2)}, u32[]{:S(2)}) collective-permute-start(f32[128,2560]{1,0:T(8,128)S(1)} %bitcast.3), channel_id=1, source_target_pairs={{0,8},{8,0},{16,24},{24,16},{32,40},{40,32},{48,56},{56,48},{64,72... | collective-permute-start | bytes 3932168 | tf_op jit(solution)/shard_map/ppermute | solution.py:342
  57.5 26.8 %copy-start.6 = (f32[32,152]{1,0:T(8,128)S(1)}, f32[32,152]{1,0:T(8,128)}, u32[]{:S(2)}) copy-start(f32[32,152]{1,0:T(8,128)} %param.8) | copy-start | bytes 58372

commit v3 on v2

v3 whole, which is shorter than its diff:
```python
import functools

import jax
import jax.numpy as jnp
from jax import lax
from jax.experimental import pallas as pl
from jax.experimental.pallas import tpu as pltpu
from jax.sharding import PartitionSpec as P

BF = jnp.bfloat16
F32 = jnp.float32
I32 = jnp.int32

NV = 400
NI = 8
PER = 50
CN = 50
WIN = 512
OJ = 8
OP = 256
ABD = 152
ABP = 160
PAY = 2560
GRP = 10
SPAN = 2176
HEAD = 4224
CD = CN * NV
EDGE = CD // 128 * 128
HOPS = (0, 2, 1, 3)
PARTS = ((0, 2), (2, 6), (8, 2))
SECT = 4
VMEM_LIMIT = 24 * 1024 * 1024
COMPACT_VMEM = 56 * 1024 * 1024
SORT_VMEM = 32 * 1024 * 1024


def nt(a, b):
    return lax.dot_general(a, b, (((1,), (1,)), ((), ())), preferred_element_type=F32)


def split(x):
    hi = x.astype(BF)
    return hi, (x - hi.astype(F32)).astype(BF)


def where_in_lanes(lane, pieces):
    out = pieces[-1][1]
    for edge, x in reversed(pieces[:-1]):
        out = jnp.where(lane < edge, x, out)
    return out


def turn(lane, x):
    moved = jnp.where(lane < 62, pltpu.roll(x, 65, 1), pltpu.roll(x, 62, 1))
    return jnp.where(lane < 125, moved, 0.0)


def compact_kernel(blk, virt_s, pair_s, virt_v, amps, ints, edge, pays, four, aux, tail, head, amp, pay, sems):
    load = pltpu.make_async_copy(amps, amp, sems.at[0])
    load.start()
    ahead = pltpu.make_async_copy(ints.at[:, pl.ds(0, HEAD)], head, sems.at[1])
    ahead.start()
    c0 = blk() * CN
    lane = lax.broadcasted_iota(I32, (8, WIN), 1)
    sub = lax.broadcasted_iota(I32, (8, WIN), 0)
    irrep = jnp.concatenate([virt_v[...], jnp.full((1, WIN - NV), -1, I32)], axis=1)
    irrep = jnp.broadcast_to(irrep, (8, WIN))
    member = irrep == sub
    before = lax.broadcasted_iota(I32, (WIN, WIN), 0) < lax.broadcasted_iota(I32, (WIN, WIN), 1)
    count = jnp.dot(
        jnp.where(member, 1.0, 0.0).astype(BF),
        jnp.where(before, 1.0, 0.0).astype(BF),
        preferred_element_type=F32,
    )
    rank = jnp.sum(jnp.where(member, count, 0.0), axis=0, keepdims=True).astype(I32)
    rank = jnp.where(lane < NV, jnp.broadcast_to(rank, (8, WIN)), -1)
    tail[...] = jnp.where(lax.broadcasted_iota(I32, (ABD, 128), 1) < CD - EDGE, edge[...], 0.0)
    pair = jnp.zeros((8, WIN), I32)
    for i in range(OJ):
        pair = jnp.where(sub == i, pair_s[i], pair)
    need = jnp.where(lane < NV, jnp.bitwise_xor(irrep, pair), -1)
    row = lax.broadcasted_iota(I32, (128, WIN), 0)
    rows = {}
    load.wait()
    for v in range(8):
        need_v = pltpu.roll(need, 16 * v, 1) if v else need
        rank_v = pltpu.roll(rank, 16 * v, 1) if v else rank
        aux[v, 0:8, :] = rank_v
        aux[v, 8:16, :] = pltpu.roll(irrep, 16 * v, 1) if v else irrep
        pick = jnp.where(jnp.broadcast_to(rank_v[0:1, :], (128, WIN)) == row, 1.0, 0.0).astype(BF)
        cs = list(range(v, CN, 8))
        xs = []
        for c in cs:
            first = (NV * c) // 128 * 128
            width = min(WIN, CD - first)
            x = amp[:, first : first + width]
            if width < WIN:
                x = jnp.concatenate([x, jnp.zeros((8, WIN - width), F32)], axis=1)
            xs.append(jnp.where(need_v == virt_s[c0 + c], x, 0.0))
        if len(xs) % 2:
            xs.append(jnp.zeros((8, WIN), F32))
        hi, lo = split(jnp.concatenate(xs, axis=0))
        r = nt(hi, pick) + nt(lo, pick)
        for i, c in enumerate(cs):
            rows[c] = r[8 * i : 8 * i + 8, :]
    lane = lax.broadcasted_iota(I32, (8, 128), 1)
    odd = jnp.bitwise_and(pair[:, 0:128], 1) == 1
    for q in range(GRP):
        r0, r1, r2, r3, r4 = (rows[5 * q + e] for e in range(5))
        r1 = pltpu.roll(r1, 50, 1)
        r2a = pltpu.roll(r2, 100, 1)
        r2b = pltpu.roll(r2, 103, 1)
        r3 = pltpu.roll(r3, 25, 1)
        r4 = pltpu.roll(r4, 75, 1)
        a = where_in_lanes(lane, [(50, r0), (100, r1), (125, r2a), (128, jnp.zeros_like(r0))])
        b = where_in_lanes(lane, [(25, r2b), (75, r3), (128, r4)])
        a = jnp.where(odd, turn(lane, a), a)
        b = jnp.where(odd, turn(lane, b), b)
        if q == GRP - 1:
            b = jnp.where(lane == 127, pair[:, 0:128].astype(F32), b)
        pay[:, 256 * q : 256 * q + 128] = a
        pay[:, 256 * q + 128 : 256 * q + 256] = b
    copies = [
        pltpu.make_async_copy(pay, pays, sems.at[2]),
        pltpu.make_async_copy(pay, four.at[pl.ds(0, OJ), :], sems.at[3]),
    ]
    for c in copies:
        c.start()
    for c in copies:
        c.wait()
    ahead.wait()


def start_of(q):
    return NV * 5 * q // 128 * 128


def chunks(q0, nq):
    edges = [start_of(q0 + 2)] + [min(start_of(q) + SPAN, EDGE) for q in range(q0 + 3, q0 + nq, 2)]
    return [(a, b - a) for a, b in zip(edges, edges[1:])]


def sort_kernel(blk, q0, nq, virt_s, aux, tail, head, ints, *refs):
    lhi, llo, done = refs[:3]
    x, ba, bb, ma, mb, sems = refs[-6:]
    c0 = blk() * CN
    spans = chunks(q0, nq)
    base = start_of(q0 + 2)
    copies = [
        pltpu.make_async_copy(
            ints.at[:, pl.ds(first, width)], x.at[:, pl.ds(first - base, width)], sems.at[j]
        )
        for j, (first, width) in enumerate(spans)
    ]
    if q0 + nq < GRP:
        wide = min(HEAD, EDGE - start_of(q0 + nq))
        copies.append(pltpu.make_async_copy(ints.at[:, pl.ds(start_of(q0 + nq), wide)], refs[3].at[:, pl.ds(0, wide)], sems.at[nq // 2 - 1]))
    for c in copies:
        c.start()
    if q0 + nq == GRP and nq > 2:
        x[:, EDGE - base : EDGE - base + 128] = tail[...]
    for b in (ba, bb):
        b[ABD - 8 : ABP, :] = jnp.zeros((ABP - ABD + 8, SPAN), BF)
        b[ABP + ABD - 8 : 2 * ABP, :] = jnp.zeros((ABP - ABD + 8, SPAN), BF)
    row = lax.broadcasted_iota(I32, (128, WIN), 0)
    lane = lax.broadcasted_iota(I32, (2 * ABP, 128), 1)
    turned = jnp.where(lane < 62, lane + 63, lane - 62).astype(F32).astype(BF)
    lane = lane.astype(F32).astype(BF)

    def load(i, b):
        begin = start_of(q0 + i) - start_of(q0 + i // 2 * 2 if i < 2 else q0 + 2)
        w = (head if i < 2 else x)[:, begin : begin + SPAN]
        if q0 + i == GRP - 1 and i < 2:
            w = jnp.concatenate([w[:, : SPAN - 128], tail[...]], axis=1)
        hi, lo = split(w)
        b[0:ABD, :] = hi
        b[ABP : ABP + ABD, :] = lo

    def sort(i, e, b, m):
        start = NV * 5 * (q0 + i)
        at = start - start // 128 * 128 + NV * e
        first = at // 128 * 128
        v = (5 * (q0 + i) + e) % 8
        rank = aux[v, 0:8, :]
        irrep = aux[v, 8:16, :]
        inside = rank >= 0
        sector = jnp.bitwise_xor(irrep, virt_s[c0 + 5 * (q0 + i) + e])
        place = rank + 50 * e
        place = jnp.where(place >= 125, place - 125, place)
        place = place + 62 * jnp.bitwise_and(sector, 1)
        place = jnp.where(place >= 125, place - 125, place)
        place = jnp.where(inside, place, -1)
        pick = jnp.where(jnp.broadcast_to(place[0:1, :], (128, WIN)) == row, 1.0, 0.0).astype(BF)
        half = jnp.where(inside, lax.shift_right_logical(sector, 1), -1)
        for u in range(4):
            on = jnp.where(half[0:1, :] == u, 1.0, 0.0).astype(BF)
            m[e, 128 * u : 128 * u + 128, :] = pick * jnp.broadcast_to(on, (128, WIN))
        return nt(b[:, first : first + WIN], m[e]).astype(BF)

    def merge(i, u, parts):
        to = 256 * i
        r = [p[:, 128 * u : 128 * u + 128] for p in parts]
        for odd in range(2):
            at = turned if odd else lane
            for t in range(2):
                edges = [(50, r[0]), (100, r[1]), (128, r[2])] if t == 0 else [(25, r[2]), (75, r[3]), (128, r[4])]
                y = where_in_lanes(at, edges)
                lhi[2 * u + odd, :, to + 128 * t : to + 128 * t + 128] = y[0:ABP]
                llo[2 * u + odd, :, to + 128 * t : to + 128 * t + 128] = y[ABP : 2 * ABP]

    def pair(k):
        i = 2 * k
        if k:
            copies[k - 1].wait()
        load(i, ba)
        load(i + 1, bb)
        pa = [sort(i, e, ba, ma) for e in range(5)]
        pb = []
        for e in range(5):
            pb.append(sort(i + 1, e, bb, mb))
            if e < 4:
                merge(i, e, pa)
        for u in range(4):
            merge(i + 1, u, pb)

    for k in range(nq // 2):
        pair(k)
    for c in copies[nq // 2 - 1 :]:
        c.wait()
    done[...] = jnp.zeros_like(done)


def main_kernel(rows, widths, *refs):
    n = len(widths)
    pieces = refs[:8]
    ls = refs[8 : 8 + 2 * n]
    out, ghi, glo, acc, pair, order = refs[8 + 3 * n :]
    for j in range(8):
        x = pieces[j][...]
        hi, lo = split(x)
        ghi[32 * j : 32 * j + 32, :] = hi
        glo[32 * j : 32 * j + 32, :] = lo
    last = jnp.concatenate([p[:, PAY - 128 : PAY] for p in pieces], axis=0)
    pair[...] = jnp.transpose(last)[120:128, :]
    acc[...] = jnp.zeros_like(acc)

    def some(step, carry):
        total = None
        k = 0
        for i, w in enumerate(widths):
            hi = ls[2 * i][pl.ds(SECT * step, SECT)].reshape(SECT * ABP, w)
            lo = ls[2 * i + 1][pl.ds(SECT * step, SECT)].reshape(SECT * ABP, w)
            x = nt(hi, ghi[:, k : k + w]) + nt(lo, ghi[:, k : k + w]) + nt(hi, glo[:, k : k + w])
            total = x if total is None else total + x
            k += w
        part = acc[...]
        for i in range(SECT):
            own = jnp.broadcast_to(pair[7:8, :], (ABP, OP)) == (SECT * step + i).astype(F32)
            part = part + jnp.where(own, total[ABP * i : ABP * i + ABP, :], 0.0)
        acc[...] = part
        return carry

    lax.fori_loop(0, NI // SECT, some, 0)
    t = jnp.transpose(acc[...])
    me = rows()
    core, y, x = lax.rem(me, 2), lax.rem(me // 2, 4), me // 8
    for j in range(8):
        kind = core if j < 4 else 1 - core
        for i in range(4):
            d1, d2 = HOPS[i], HOPS[j % 4]
            dx = jnp.where(kind == 0, d1, d2)
            dy = jnp.where(kind == 0, d2, d1)
            shard = (lax.rem(x + 4 - dx, 4) * 4 + lax.rem(y + 4 - dy, 4)) * 2 + kind
            to = pl.multiple_of(shard * OJ, OJ)
            order[pl.ds(to, OJ), :] = t[32 * j + 8 * i : 32 * j + 8 * i + 8, :]
    for b in range(8):
        out[b, 0:32, :] = order[32 * b : 32 * b + 32, 0:128]
        rest = [order[32 * b + 8 * g : 32 * b + 8 * g + 8, 128:ABP] for g in range(4)]
        out[b, 32:40, :] = jnp.concatenate(rest, axis=1)


def finish(got, resid):
    total = jnp.sum(got, axis=0)
    rest = [total[32:40, 32 * g : 32 * g + ABD - 128] for g in range(4)]
    return resid + jnp.concatenate([total[0:32], jnp.concatenate(rest, axis=0)], axis=1)


def smem():
    return pl.BlockSpec(memory_space=pltpu.SMEM)


def in_hbm(x):
    return pltpu.with_memory_space_constraint(x, pltpu.HBM)


def whole(shape):
    return pl.BlockSpec(shape, lambda g: (0,) * len(shape))


def compact(blk, virt, pair, amp, ints):
    hbm = pl.BlockSpec(memory_space=pltpu.HBM)
    return pl.pallas_call(
        functools.partial(compact_kernel, blk),
        out_shape=(
            jax.ShapeDtypeStruct((OJ, PAY), F32),
            jax.ShapeDtypeStruct((4 * OJ, PAY), F32),
            pltpu.VMEM((8, 16, WIN), I32),
            pltpu.VMEM((ABD, 128), F32),
            pltpu.VMEM((ABD, HEAD), F32),
        ),
        grid=(1,),
        in_specs=[
            smem(),
            smem(),
            whole((1, NV)),
            hbm,
            hbm,
            pl.BlockSpec((ABD, 128), lambda g: (0, EDGE // 128)),
        ],
        out_specs=(
            pl.BlockSpec(memory_space=pl.ANY),
            pl.BlockSpec(memory_space=pl.ANY),
            whole((8, 16, WIN)),
            whole((ABD, 128)),
            pl.BlockSpec(memory_space=pl.ANY),
        ),
        scratch_shapes=[pltpu.VMEM((OJ, CD), F32), pltpu.VMEM((OJ, PAY), F32), pltpu.SemaphoreType.DMA((4,))],
        compiler_params=pltpu.CompilerParams(vmem_limit_bytes=COMPACT_VMEM),
        name="compact",
    )(virt, pair, virt.reshape(1, NV), in_hbm(amp), in_hbm(ints), in_hbm(ints))


def sort_part(blk, q0, nq, virt, aux, tail, head, ints):
    shape = pltpu.VMEM((NI, ABP, 256 * nq), BF)
    vmem = pl.BlockSpec(memory_space=pltpu.VMEM)
    more = q0 + nq < GRP
    return pl.pallas_call(
        functools.partial(sort_kernel, blk, q0, nq),
        out_shape=(shape, shape, pltpu.VMEM((8, 128), F32)) + (pltpu.VMEM((ABD, HEAD), F32),) * more,
        in_specs=[smem(), vmem, vmem, vmem, pl.BlockSpec(memory_space=pltpu.HBM)],
        out_specs=(vmem,) * (3 + more),
        scratch_shapes=[
            pltpu.VMEM((ABD, max(start_of(q0 + nq - 1) + SPAN - start_of(q0 + 2), 128)), F32),
            pltpu.VMEM((2 * ABP, SPAN), BF),
            pltpu.VMEM((2 * ABP, SPAN), BF),
            pltpu.VMEM((5, 512, WIN), BF),
            pltpu.VMEM((5, 512, WIN), BF),
            pltpu.SemaphoreType.DMA((nq // 2,)),
        ],
        compiler_params=pltpu.CompilerParams(vmem_limit_bytes=SORT_VMEM),
        cost_estimate=pl.CostEstimate(flops=nq * 5 * 2 * 320 * 512 * 512, bytes_accessed=nq * 1300000, transcendentals=0),
        name="sort_ints",
    )(virt, aux, tail, head, in_hbm(ints))


def contract(rows, pieces, parts):
    widths = tuple(p[0].shape[2] for p in parts)
    flat = [x for p in parts for x in p[:2]]
    vmem = pl.BlockSpec(memory_space=pltpu.VMEM)
    hbm = pl.BlockSpec(memory_space=pl.ANY)
    return pl.pallas_call(
        functools.partial(main_kernel, rows, widths),
        out_shape=jax.ShapeDtypeStruct((8, 40, 128), F32),
        in_specs=[vmem] * (8 + len(flat)) + [hbm] * len(parts),
        out_specs=vmem,
        scratch_shapes=[
            pltpu.VMEM((OP, PAY), BF),
            pltpu.VMEM((OP, PAY), BF),
            pltpu.VMEM((ABP, OP), F32),
            pltpu.VMEM((8, OP), F32),
            pltpu.VMEM((OP, ABP), F32),
        ],
        compiler_params=pltpu.CompilerParams(vmem_limit_bytes=VMEM_LIMIT),
        cost_estimate=pl.CostEstimate(flops=3 * 2 * 1280 * 2560 * 256, bytes_accessed=16000000, transcendentals=0),
        name="contract",
    )(*pieces, *[pltpu.with_memory_space_constraint(x, pltpu.VMEM) for x in flat], *[p[2] for p in parts])


def at(x, y, core):
    return ((x % 4) * 4 + y % 4) * 2 + core


def walk(hop, second):
    pairs = []
    for x in range(4):
        for y in range(4):
            for core in range(2):
                along_x = (core == 0) != second
                to = at(x + hop, y, core) if along_x else at(x, y + hop, core)
                pairs.append((at(x, y, core), to))
    return pairs


SWAP = [(i, i ^ 1) for i in range(32)]


def body(amplitudes, pair_irrep, virt_irrep, resid_in, ladder_ints):
    blk = functools.partial(lax.axis_index, "blk")
    hold = lax.optimization_barrier
    pay, four, aux, tail, head = compact(blk, virt_irrep, pair_irrep, amplitudes, ladder_ints)

    def sort(q0, nq, aux, head):
        return list(sort_part(blk, q0, nq, virt_irrep, aux, tail, head, ladder_ints))

    line = [lax.ppermute(pay, "rows", walk(h, False)) for h in HOPS[1:]]
    parts = [sort(*PARTS[0], aux, head)]
    line, parts[0][2], aux = hold((line, parts[0][2], aux))
    for i, x in enumerate(line):
        four = lax.dynamic_update_slice(four, x, (OJ * (i + 1), 0))
    near = [lax.ppermute(four, "rows", walk(h, True)) for h in HOPS[1:]]
    far = [lax.ppermute(four, "rows", SWAP)]
    parts.append(sort(*PARTS[1], aux, parts[0][3]))
    near, parts[1][2], aux = hold((near, parts[1][2], aux))
    far += [lax.ppermute(p, "rows", SWAP) for p in near]
    parts.append(sort(*PARTS[2], aux, parts[1][3]))
    terms = contract(functools.partial(lax.axis_index, "rows"), [four] + near + far, parts)
    return finish(lax.all_to_all(terms, "blk", 0, 0), resid_in)


def solution(mesh):
    placed = (P("rows", "blk"), P("rows"), P(), P("blk", "rows"), P("rows", "blk"))
    return jax.shard_map(
        body, mesh=mesh, in_specs=placed, out_specs=P("blk", "rows"), check_vma=False
    )
```

time: 85.2 us -> 57.7 us (0.68)
  the two profiles are of different devices: /device:TPU:1 before, /device:TPU:6 now
where the time goes in v3:
time: 57.7 us; the launch traced here: 57.5 us
  Pallas kernels  24.1 us (42%)
  blocking collectives  18.3 us (32%)
  starting transfers between devices  11.2 us (19%)
  waiting for transfers between devices  3 us (5%)
  other arithmetic  0.64 us (1%)
    all_to_all x1, blocking collectives, body(): return finish(lax.all_to_all(terms, 'blk', 0, 0), resid_in)  18.3 us
    pallas_call x3, Pallas kernels, sort_part(): pl.pallas_call(functools.partial(sort_kernel, blk, q0, nq), out_shape=(sh...  13.9 us
    ppermute x3, starting transfers between devices, body(): near = [lax.ppermute(four, 'rows', walk(h, True)) for h in HOPS[1:]]  6.52 us
    pallas_call x1, Pallas kernels, contract(): pl.pallas_call(functools.partial(main_kernel, rows, widths), out_shape=ja...  6.4 us
    pallas_call x1, Pallas kernels, compact(): pl.pallas_call(functools.partial(compact_kernel, blk), out_shape=(jax.Sha...  3.79 us
    ppermute x3, starting transfers between devices, body(): line = [lax.ppermute(pay, 'rows', walk(h, False)) for h in HOPS[1:]]  3.59 us
    ppermute x3, waiting for transfers between devices, body(): line = [lax.ppermute(pay, 'rows', walk(h, False)) for h in HOPS[1:]]  2.98 us
  transfers between devices with their start and end apart: 10, of which 2 were waited for; matrix products, arithmetic and copies ran while one was open for 0% of the time, Pallas kernels for 24%

profile of v3, /device:TPU:6, one launch (start us, length us, event | category | flops | bytes accessed | tf_op | source)
XLA Modules:
  0.0 57.5 jit_solution(15195730527552433532)
XLA Ops:
  0.0 3.8 %compact.1 = (f32[8,2560]{1,0:T(8,128)}, f32[32,2560]{1,0:T(8,128)}, s32[8,16,512]{2,1,0:T(8,128)S(1)}, f32[152,128]{1,0:T(8,128)S(1)}, f32[152,4224]{1,0:T(8,128)S(1)}) custom-call(s32[400]{0:T(512)} %virt_s.7, s32[8]{0:T(128)} %pair_s.1, s32[1,400]{1,0:T(1,128)} %bitcast.1, f32[8,20000]{1,0:T(8,128)} %amps.1, f32[152,20000]{1,0:T(8,128)} %ints.7, ...), custom_call_target="tpu_custom_call" | custom-call | tf_op jit(solution)/shard_map/compact/pallas_call | solution.py:302
  3.8 1.5 %collective-permute-start = (f32[8,2560]{1,0:T(8,128)}, f32[8,2560]{1,0:T(8,128)S(1)}, u32[]{:S(2)}, u32[]{:S(2)}) collective-permute-start(f32[8,2560]{1,0:T(8,128)} %get-tuple-element.32), channel_id=1, source_target_pairs={{0,128},{8,40},{16,144},{24,56},{32,160},{40,8},{48,176},{56,24},{... | collective-permute-start | bytes 245768 | tf_op jit(solution)/shard_map/ppermute | solution.py:405
  5.3 2.1 %collective-permute-start.1 = (f32[8,2560]{1,0:T(8,128)}, f32[8,2560]{1,0:T(8,128)S(1)}, u32[]{:S(2)}, u32[]{:S(2)}) collective-permute-start(f32[8,2560]{1,0:T(8,128)} %get-tuple-element.32), channel_id=1, source_target_pairs={{0,64},{8,24},{16,80},{24,40},{32,96},{40,56},{48,112},{56,8},{64,... | collective-permute-start | bytes 245768 | tf_op jit(solution)/shard_map/ppermute | solution.py:405
  7.4 0.0 collective-permute-start.2
  7.4 0.0 copy-done
  7.4 2.9 %sort_ints.3 = (bf16[8,160,512]{2,1,0:T(8,128)(2,1)S(1)}, bf16[8,160,512]{2,1,0:T(8,128)(2,1)S(1)}, f32[8,128]{1,0:T(8,128)S(1)}, f32[152,4224]{1,0:T(8,128)S(1)}) custom-call(s32[400]{0:T(512)S(1)} %copy-done, s32[8,16,512]{2,1,0:T(8,128)S(1)} %get-tuple-element.50.aux, f32[152,128]{1,0:T(8,128)S(1)} %get-tuple-element.34.tail, ...), custom_call_target="tpu_custom_call" | custom-call | flops 1677721600 | bytes 2600000 | tf_op jit(solution)/shard_map/sort_ints/pallas_call | solution.py:337
  10.3 0.0 collective-permute-done
  10.3 0.2 collective-permute-done.1
  10.5 2.8 %collective-permute-done.2 = f32[8,2560]{1,0:T(8,128)S(1)} collective-permute-done((f32[8,2560]{1,0:T(8,128)}, f32[8,2560]{1,0:T(8,128)S(1)}, u32[]{:S(2)}, u32[]{:S(2)}) %collective-permute-start.2) | collective-permute-done | bytes 81952 | tf_op jit(solution)/shard_map/ppermute | solution.py:405
  13.2 0.0 copy-done.1
  13.3 3.3 %collective-permute-start.3 = (f32[32,2560]{1,0:T(8,128)S(1)}, f32[32,2560]{1,0:T(8,128)S(1)}, u32[]{:S(2)}, u32[]{:S(2)}) collective-permute-start(f32[32,2560]{1,0:T(8,128)S(1)} %constant_dynamic-update-slice_fusion.refs_0_), channel_id=1, source_target_pairs={{0,32},{8,136},{16,48},{24,152},{32,0},{40,168},{48,16},{56,184},{... | collective-permute-start | bytes 983048 | tf_op jit(solution)/shard_map/ppermute | solution.py:410
  16.6 0.7 %collective-permute-start.4 = (f32[32,2560]{1,0:T(8,128)S(1)}, f32[32,2560]{1,0:T(8,128)S(1)}, u32[]{:S(2)}, u32[]{:S(2)}) collective-permute-start(f32[32,2560]{1,0:T(8,128)S(1)} %constant_dynamic-update-slice_fusion.refs_0_), channel_id=1, source_target_pairs={{0,16},{8,72},{16,32},{24,88},{32,48},{40,104},{48,0},{56,120},{64... | collective-permute-start | bytes 983048 | tf_op jit(solution)/shard_map/ppermute | solution.py:410
  17.3 2.6 %collective-permute-start.5 = (f32[32,2560]{1,0:T(8,128)S(1)}, f32[32,2560]{1,0:T(8,128)S(1)}, u32[]{:S(2)}, u32[]{:S(2)}) collective-permute-start(f32[32,2560]{1,0:T(8,128)S(1)} %constant_dynamic-update-slice_fusion.refs_0_), channel_id=1, source_target_pairs={{0,48},{8,200},{16,0},{24,216},{32,16},{40,232},{48,32},{56,248},{... | collective-permute-start | bytes 983048 | tf_op jit(solution)/shard_map/ppermute | solution.py:410
  19.8 0.0 collective-permute-start.6
  19.8 8.2 %sort_ints.4 = (bf16[8,160,1536]{2,1,0:T(8,128)(2,1)S(1)}, bf16[8,160,1536]{2,1,0:T(8,128)(2,1)S(1)}, f32[8,128]{1,0:T(8,128)S(1)}, f32[152,4224]{1,0:T(8,128)S(1)}) custom-call(s32[400]{0:T(512)S(1)} %copy-done, s32[8,16,512]{2,1,0:T(8,128)S(1)} %get-tuple-element.50.aux, f32[152,128]{1,0:T(8,128)S(1)} %get-tuple-element.34.tail, ...), custom_call_target="tpu_custom_call" | custom-call | flops 5033164800 | bytes 7800000 | tf_op jit(solution)/shard_map/sort_ints/pallas_call | solution.py:337
  28.1 0.0 collective-permute-done.3.refs_1_
  28.1 0.0 collective-permute-done.4.refs_2_
  28.1 0.0 collective-permute-done.5.refs_3_
  28.1 0.6 %collective-permute-start.7 = (f32[32,2560]{1,0:T(8,128)S(1)}, f32[32,2560]{1,0:T(8,128)S(1)}, u32[]{:S(2)}, u32[]{:S(2)}) collective-permute-start(f32[32,2560]{1,0:T(8,128)S(1)} %collective-permute-done.3.refs_1_), channel_id=1, source_target_pairs={{0,8},{8,0},{16,24},{24,16},{32,40},{40,32},{48,56},{56,48},{64,72... | collective-permute-start | bytes 983048 | tf_op jit(solution)/shard_map/ppermute | solution.py:414
  28.7 0.1 collective-permute-start.8
  28.8 0.4 collective-permute-start.9
  29.2 2.8 %sort_ints.5 = (bf16[8,160,512]{2,1,0:T(8,128)(2,1)S(1)}, bf16[8,160,512]{2,1,0:T(8,128)(2,1)S(1)}, f32[8,128]{1,0:T(8,128)S(1)}) custom-call(s32[400]{0:T(512)S(1)} %copy-done, s32[8,16,512]{2,1,0:T(8,128)S(1)} %get-tuple-element.50.aux, f32[152,128]{1,0:T(8,128)S(1)} %get-tuple-element.34.tail, f32[152,4224]{1,0:T(8,128)S(1)} %get-tuple-element.51.head, ...), custom_call_target="tpu_custom_call" | custom-call | flops 1677721600 | bytes 2600000 | tf_op jit(solution)/shard_map/sort_ints/pallas_call | solution.py:337
  32.0 0.0 collective-permute-done.6.refs_4_
  32.1 0.0 collective-permute-done.7.refs_5_
  32.1 0.0 collective-permute-done.8.refs_6_
  32.1 0.0 collective-permute-done.9.refs_7_
  32.1 0.0 copy-start.2
  32.1 6.4 %contract.1 = f32[8,40,128]{2,1,0:T(8,128)S(1)} custom-call(f32[32,2560]{1,0:T(8,128)S(1)} %constant_dynamic-update-slice_fusion.refs_0_, f32[32,2560]{1,0:T(8,128)S(1)} %collective-permute-done.3.refs_1_, f32[32,2560]{1,0:T(8,128)S(1)} %collective-permute-done.4.refs_2_, f32[32,2560]{1,0:T(8,128)S(1)} %collective-permute-done.5.refs_3_, ...), custom_call_target="tpu_custom_call" | custom-call | flops 5033164800 | bytes 16000000 | tf_op jit(solution)/shard_map/contract/pallas_call | solution.py:361
  38.5 18.3 %all_to_all.5 = f32[8,40,128]{2,1,0:T(8,128)S(1)} all-to-all(f32[8,40,128]{2,1,0:T(8,128)S(1)} %contract.1), channel_id=1, replica_groups=mesh['rows'=32,'blk'=8] {'blk'}, dimensions={0} | all-to-all | bytes 327680 | tf_op jit(solution)/shard_map/all_to_all | solution.py:417
  56.8 0.1 fusion
  56.9 0.0 copy-done.2
  56.9 0.6 %maximum_add_fusion = f32[32,152]{1,0:T(8,128)} fusion(f32[32,152]{1,0:T(8,128)S(1)} %copy-done.2, f32[8,24]{1,0:T(8,128)S(1)} %get-tuple-element.58, f32[8,24]{1,0:T(8,128)S(1)} %get-tuple-element.59, f32[8,24]{1,0:T(8,128)S(1)} %get-tuple-element.60, f32[8,24]{1,0:T(8,128)S(1)} %get-tuple-element.57, f32[32,128]{1,0:T(8,128)S(1)} %slice.20), kind=kLoop, calls=%fused_computation | loop fusion | flops 24320 | bytes 58368 | tf_op jit(solution)/shard_map/add | solution.py:285
  (7 shorter events, 0.0 us)
Async XLA Ops:
  0.0 7.4 %copy-start = (s32[400]{0:T(512)S(1)}, s32[400]{0:T(512)}, u32[]{:S(2)}) copy-start(s32[400]{0:T(512)} %virt_s.7) | copy-start | bytes 4804
  3.8 6.5 %collective-permute-start = (f32[8,2560]{1,0:T(8,128)}, f32[8,2560]{1,0:T(8,128)S(1)}, u32[]{:S(2)}, u32[]{:S(2)}) collective-permute-start(f32[8,2560]{1,0:T(8,128)} %get-tuple-element.32), channel_id=1, source_target_pairs={{0,128},{8,40},{16,144},{24,56},{32,160},{40,8},{48,176},{56,24},{... | collective-permute-start | bytes 245768 | tf_op jit(solution)/shard_map/ppermute | solution.py:405
  5.3 5.2 %collective-permute-start.1 = (f32[8,2560]{1,0:T(8,128)}, f32[8,2560]{1,0:T(8,128)S(1)}, u32[]{:S(2)}, u32[]{:S(2)}) collective-permute-start(f32[8,2560]{1,0:T(8,128)} %get-tuple-element.32), channel_id=1, source_target_pairs={{0,64},{8,24},{16,80},{24,40},{32,96},{40,56},{48,112},{56,8},{64,... | collective-permute-start | bytes 245768 | tf_op jit(solution)/shard_map/ppermute | solution.py:405
  7.4 5.9 %collective-permute-start.2 = (f32[8,2560]{1,0:T(8,128)}, f32[8,2560]{1,0:T(8,128)S(1)}, u32[]{:S(2)}, u32[]{:S(2)}) collective-permute-start(f32[8,2560]{1,0:T(8,128)} %get-tuple-element.32), channel_id=1, source_target_pairs={{0,192},{8,56},{16,208},{24,8},{32,224},{40,24},{48,240},{56,40},{... | collective-permute-start | bytes 245768 | tf_op jit(solution)/shard_map/ppermute | solution.py:405
  7.4 5.9 %copy-start.1 = (f32[32,2560]{1,0:T(8,128)S(1)}, f32[32,2560]{1,0:T(8,128)}, u32[]{:S(2)}) copy-start(f32[32,2560]{1,0:T(8,128)} %get-tuple-element.31) | copy-start | bytes 983044
  13.3 14.8 %collective-permute-start.3 = (f32[32,2560]{1,0:T(8,128)S(1)}, f32[32,2560]{1,0:T(8,128)S(1)}, u32[]{:S(2)}, u32[]{:S(2)}) collective-permute-start(f32[32,2560]{1,0:T(8,128)S(1)} %constant_dynamic-update-slice_fusion.refs_0_), channel_id=1, source_target_pairs={{0,32},{8,136},{16,48},{24,152},{32,0},{40,168},{48,16},{56,184},{... | collective-permute-start | bytes 983048 | tf_op jit(solution)/shard_map/ppermute | solution.py:410
  16.6 11.5 %collective-permute-start.4 = (f32[32,2560]{1,0:T(8,128)S(1)}, f32[32,2560]{1,0:T(8,128)S(1)}, u32[]{:S(2)}, u32[]{:S(2)}) collective-permute-start(f32[32,2560]{1,0:T(8,128)S(1)} %constant_dynamic-update-slice_fusion.refs_0_), channel_id=1, source_target_pairs={{0,16},{8,72},{16,32},{24,88},{32,48},{40,104},{48,0},{56,120},{64... | collective-permute-start | bytes 983048 | tf_op jit(solution)/shard_map/ppermute | solution.py:410
  17.3 10.8 %collective-permute-start.5 = (f32[32,2560]{1,0:T(8,128)S(1)}, f32[32,2560]{1,0:T(8,128)S(1)}, u32[]{:S(2)}, u32[]{:S(2)}) collective-permute-start(f32[32,2560]{1,0:T(8,128)S(1)} %constant_dynamic-update-slice_fusion.refs_0_), channel_id=1, source_target_pairs={{0,48},{8,200},{16,0},{24,216},{32,16},{40,232},{48,32},{56,248},{... | collective-permute-start | bytes 983048 | tf_op jit(solution)/shard_map/ppermute | solution.py:410
  19.8 12.2 %collective-permute-start.6 = (f32[32,2560]{1,0:T(8,128)S(1)}, f32[32,2560]{1,0:T(8,128)S(1)}, u32[]{:S(2)}, u32[]{:S(2)}) collective-permute-start(f32[32,2560]{1,0:T(8,128)S(1)} %constant_dynamic-update-slice_fusion.refs_0_), channel_id=1, source_target_pairs={{0,8},{8,0},{16,24},{24,16},{32,40},{40,32},{48,56},{56,48},{64,72... | collective-permute-start | bytes 983048 | tf_op jit(solution)/shard_map/ppermute | solution.py:411
  28.1 4.0 %collective-permute-start.7 = (f32[32,2560]{1,0:T(8,128)S(1)}, f32[32,2560]{1,0:T(8,128)S(1)}, u32[]{:S(2)}, u32[]{:S(2)}) collective-permute-start(f32[32,2560]{1,0:T(8,128)S(1)} %collective-permute-done.3.refs_1_), channel_id=1, source_target_pairs={{0,8},{8,0},{16,24},{24,16},{32,40},{40,32},{48,56},{56,48},{64,72... | collective-permute-start | bytes 983048 | tf_op jit(solution)/shard_map/ppermute | solution.py:414
  28.7 3.4 %collective-permute-start.8 = (f32[32,2560]{1,0:T(8,128)S(1)}, f32[32,2560]{1,0:T(8,128)S(1)}, u32[]{:S(2)}, u32[]{:S(2)}) collective-permute-start(f32[32,2560]{1,0:T(8,128)S(1)} %collective-permute-done.4.refs_2_), channel_id=1, source_target_pairs={{0,8},{8,0},{16,24},{24,16},{32,40},{40,32},{48,56},{56,48},{64,72... | collective-permute-start | bytes 983048 | tf_op jit(solution)/shard_map/ppermute | solution.py:414
  28.8 3.3 %collective-permute-start.9 = (f32[32,2560]{1,0:T(8,128)S(1)}, f32[32,2560]{1,0:T(8,128)S(1)}, u32[]{:S(2)}, u32[]{:S(2)}) collective-permute-start(f32[32,2560]{1,0:T(8,128)S(1)} %collective-permute-done.5.refs_3_), channel_id=1, source_target_pairs={{0,8},{8,0},{16,24},{24,16},{32,40},{40,32},{48,56},{56,48},{64,72... | collective-permute-start | bytes 983048 | tf_op jit(solution)/shard_map/ppermute | solution.py:414
  32.1 24.8 %copy-start.2 = (f32[32,152]{1,0:T(8,128)S(1)}, f32[32,152]{1,0:T(8,128)}, u32[]{:S(2)}) copy-start(f32[32,152]{1,0:T(8,128)} %param.8) | copy-start | bytes 58372

commit v4 on v3

--- a/solution.py
+++ b/solution.py
@@ -20,6 +20,7 @@
 OP = 256
 ABD = 152
 ABP = 160
+ABS = 2 * ABD
 PAY = 2560
 GRP = 10
 SPAN = 2176
@@ -31,7 +32,7 @@
 SECT = 4
 VMEM_LIMIT = 24 * 1024 * 1024
 COMPACT_VMEM = 56 * 1024 * 1024
-SORT_VMEM = 32 * 1024 * 1024
+SORT_VMEM = 22 * 1024 * 1024
 
 
 def nt(a, b):
@@ -55,11 +56,7 @@
     return jnp.where(lane < 125, moved, 0.0)
 
 
-def compact_kernel(blk, virt_s, pair_s, virt_v, amps, ints, edge, pays, four, aux, tail, head, amp, pay, sems):
-    load = pltpu.make_async_copy(amps, amp, sems.at[0])
-    load.start()
-    ahead = pltpu.make_async_copy(ints.at[:, pl.ds(0, HEAD)], head, sems.at[1])
-    ahead.start()
+def compact_kernel(blk, virt_s, pair_s, virt_v, amp, edge, pays, four, aux, tail, pay, sems):
     c0 = blk() * CN
     lane = lax.broadcasted_iota(I32, (8, WIN), 1)
     sub = lax.broadcasted_iota(I32, (8, WIN), 0)
@@ -81,7 +78,6 @@
     need = jnp.where(lane < NV, jnp.bitwise_xor(irrep, pair), -1)
     row = lax.broadcasted_iota(I32, (128, WIN), 0)
     rows = {}
-    load.wait()
     for v in range(8):
         need_v = pltpu.roll(need, 16 * v, 1) if v else need
         rank_v = pltpu.roll(rank, 16 * v, 1) if v else rank
@@ -121,14 +117,13 @@
         pay[:, 256 * q : 256 * q + 128] = a
         pay[:, 256 * q + 128 : 256 * q + 256] = b
     copies = [
-        pltpu.make_async_copy(pay, pays, sems.at[2]),
-        pltpu.make_async_copy(pay, four.at[pl.ds(0, OJ), :], sems.at[3]),
+        pltpu.make_async_copy(pay, pays, sems.at[0]),
+        pltpu.make_async_copy(pay, four.at[pl.ds(0, OJ), :], sems.at[1]),
     ]
     for c in copies:
         c.start()
     for c in copies:
         c.wait()
-    ahead.wait()
 
 
 def start_of(q):
@@ -140,8 +135,12 @@
     return [(a, b - a) for a, b in zip(edges, edges[1:])]
 
 
-def sort_kernel(blk, q0, nq, virt_s, aux, tail, head, ints, *refs):
-    lhi, llo, done = refs[:3]
+def sort_kernel(blk, q0, nq, virt_s, aux, tail, ints, *refs):
+    if q0:
+        head, *refs = refs
+    else:
+        *refs, head, head_sems = refs
+    both, done = refs[:2]
     x, ba, bb, ma, mb, sems = refs[-6:]
     c0 = blk() * CN
     spans = chunks(q0, nq)
@@ -154,16 +153,19 @@
     ]
     if q0 + nq < GRP:
         wide = min(HEAD, EDGE - start_of(q0 + nq))
-        copies.append(pltpu.make_async_copy(ints.at[:, pl.ds(start_of(q0 + nq), wide)], refs[3].at[:, pl.ds(0, wide)], sems.at[nq // 2 - 1]))
-    for c in copies:
+        copies.append(pltpu.make_async_copy(ints.at[:, pl.ds(start_of(q0 + nq), wide)], refs[2].at[:, pl.ds(0, wide)], sems.at[nq // 2 - 1]))
+    first = []
+    if not q0:
+        first = [
+            pltpu.make_async_copy(ints.at[:, pl.ds(a, w)], head.at[:, pl.ds(a, w)], head_sems.at[j])
+            for j, (a, w) in enumerate(((0, SPAN), (SPAN, HEAD - SPAN)))
+        ]
+    for c in first + copies:
         c.start()
     if q0 + nq == GRP and nq > 2:
         x[:, EDGE - base : EDGE - base + 128] = tail[...]
-    for b in (ba, bb):
-        b[ABD - 8 : ABP, :] = jnp.zeros((ABP - ABD + 8, SPAN), BF)
-        b[ABP + ABD - 8 : 2 * ABP, :] = jnp.zeros((ABP - ABD + 8, SPAN), BF)
     row = lax.broadcasted_iota(I32, (128, WIN), 0)
-    lane = lax.broadcasted_iota(I32, (2 * ABP, 128), 1)
+    lane = lax.broadcasted_iota(I32, (ABS, 128), 1)
     turned = jnp.where(lane < 62, lane + 63, lane - 62).astype(F32).astype(BF)
     lane = lane.astype(F32).astype(BF)
 
@@ -172,9 +174,8 @@
         w = (head if i < 2 else x)[:, begin : begin + SPAN]
         if q0 + i == GRP - 1 and i < 2:
             w = jnp.concatenate([w[:, : SPAN - 128], tail[...]], axis=1)
-        hi, lo = split(w)
-        b[0:ABD, :] = hi
-        b[ABP : ABP + ABD, :] = lo
+        hi = w.astype(BF).astype(F32)
+        b[...] = jnp.concatenate([hi, w - hi], axis=0).astype(BF)
 
     def sort(i, e, b, m):
         start = NV * 5 * (q0 + i)
@@ -205,16 +206,23 @@
             for t in range(2):
                 edges = [(50, r[0]), (100, r[1]), (128, r[2])] if t == 0 else [(25, r[2]), (75, r[3]), (128, r[4])]
                 y = where_in_lanes(at, edges)
-                lhi[2 * u + odd, :, to + 128 * t : to + 128 * t + 128] = y[0:ABP]
-                llo[2 * u + odd, :, to + 128 * t : to + 128 * t + 128] = y[ABP : 2 * ABP]
+                both[2 * u + odd, :, to + 128 * t : to + 128 * t + 128] = y
 
     def pair(k):
         i = 2 * k
         if k:
             copies[k - 1].wait()
-        load(i, ba)
-        load(i + 1, bb)
-        pa = [sort(i, e, ba, ma) for e in range(5)]
+        if first and not k:
+            first[0].wait()
+            load(i, ba)
+            pa = [sort(i, e, ba, ma) for e in range(2)]
+            first[1].wait()
+            load(i + 1, bb)
+            pa += [sort(i, e, ba, ma) for e in range(2, 5)]
+        else:
+            load(i, ba)
+            load(i + 1, bb)
+            pa = [sort(i, e, ba, ma) for e in range(5)]
         pb = []
         for e in range(5):
             pb.append(sort(i + 1, e, bb, mb))
@@ -233,8 +241,8 @@
 def main_kernel(rows, widths, *refs):
     n = len(widths)
     pieces = refs[:8]
-    ls = refs[8 : 8 + 2 * n]
-    out, ghi, glo, acc, pair, order = refs[8 + 3 * n :]
+    ls = refs[8 : 8 + n]
+    out, ghi, glo, acc, pair, order = refs[8 + 2 * n :]
     for j in range(8):
         x = pieces[j][...]
         hi, lo = split(x)
@@ -248,20 +256,21 @@
         total = None
         k = 0
         for i, w in enumerate(widths):
-            hi = ls[2 * i][pl.ds(SECT * step, SECT)].reshape(SECT * ABP, w)
-            lo = ls[2 * i + 1][pl.ds(SECT * step, SECT)].reshape(SECT * ABP, w)
-            x = nt(hi, ghi[:, k : k + w]) + nt(lo, ghi[:, k : k + w]) + nt(hi, glo[:, k : k + w])
-            total = x if total is None else total + x
+            both = ls[i][pl.ds(SECT * step, SECT)]
+            x = nt(both.reshape(SECT * ABS, w), ghi[:, k : k + w])
+            y = nt(both[:, 0:ABP].reshape(SECT * ABP, w), glo[:, k : k + w])
+            total = (x, y) if total is None else (total[0] + x, total[1] + y)
             k += w
         part = acc[...]
         for i in range(SECT):
-            own = jnp.broadcast_to(pair[7:8, :], (ABP, OP)) == (SECT * step + i).astype(F32)
-            part = part + jnp.where(own, total[ABP * i : ABP * i + ABP, :], 0.0)
+            x, y = total[0][ABS * i : ABS * i + ABS], total[1][ABP * i : ABP * i + ABD]
+            own = jnp.broadcast_to(pair[7:8, :], (ABD, OP)) == (SECT * step + i).astype(F32)
+            part = part + jnp.where(own, x[0:ABD] + x[ABD:ABS] + y, 0.0)
         acc[...] = part
         return carry
 
     lax.fori_loop(0, NI // SECT, some, 0)
-    t = jnp.transpose(acc[...])
+    t = jnp.transpose(jnp.concatenate([acc[...], jnp.zeros((ABP - ABD, OP), F32)], axis=0))
     me = rows()
     core, y, x = lax.rem(me, 2), lax.rem(me // 2, 4), me // 8
     for j in range(8):
@@ -298,23 +307,20 @@
 
 
 def compact(blk, virt, pair, amp, ints):
-    hbm = pl.BlockSpec(memory_space=pltpu.HBM)
     return pl.pallas_call(
         functools.partial(compact_kernel, blk),
         out_shape=(
-            jax.ShapeDtypeStruct((OJ, PAY), F32),
-            jax.ShapeDtypeStruct((4 * OJ, PAY), F32),
+            pltpu.VMEM((OJ, PAY), F32),
+            pltpu.VMEM((4 * OJ, PAY), F32),
             pltpu.VMEM((8, 16, WIN), I32),
             pltpu.VMEM((ABD, 128), F32),
-            pltpu.VMEM((ABD, HEAD), F32),
         ),
         grid=(1,),
         in_specs=[
             smem(),
             smem(),
             whole((1, NV)),
-            hbm,
-            hbm,
+            whole((OJ, CD)),
             pl.BlockSpec((ABD, 128), lambda g: (0, EDGE // 128)),
         ],
         out_specs=(
@@ -322,40 +328,41 @@
             pl.BlockSpec(memory_space=pl.ANY),
             whole((8, 16, WIN)),
             whole((ABD, 128)),
-            pl.BlockSpec(memory_space=pl.ANY),
         ),
-        scratch_shapes=[pltpu.VMEM((OJ, CD), F32), pltpu.VMEM((OJ, PAY), F32), pltpu.SemaphoreType.DMA((4,))],
+        scratch_shapes=[pltpu.VMEM((OJ, PAY), F32), pltpu.SemaphoreType.DMA((2,))],
         compiler_params=pltpu.CompilerParams(vmem_limit_bytes=COMPACT_VMEM),
         name="compact",
-    )(virt, pair, virt.reshape(1, NV), in_hbm(amp), in_hbm(ints), in_hbm(ints))
+    )(virt, pair, virt.reshape(1, NV), in_hbm(amp), in_hbm(ints))
 
 
 def sort_part(blk, q0, nq, virt, aux, tail, head, ints):
-    shape = pltpu.VMEM((NI, ABP, 256 * nq), BF)
+    shape = pltpu.VMEM((NI, ABS, 256 * nq), BF)
     vmem = pl.BlockSpec(memory_space=pltpu.VMEM)
     more = q0 + nq < GRP
+    heads = [head] if q0 else []
     return pl.pallas_call(
         functools.partial(sort_kernel, blk, q0, nq),
-        out_shape=(shape, shape, pltpu.VMEM((8, 128), F32)) + (pltpu.VMEM((ABD, HEAD), F32),) * more,
-        in_specs=[smem(), vmem, vmem, vmem, pl.BlockSpec(memory_space=pltpu.HBM)],
-        out_specs=(vmem,) * (3 + more),
+        out_shape=(shape, pltpu.VMEM((8, 128), F32)) + (pltpu.VMEM((ABD, HEAD), F32),) * more,
+        in_specs=[smem(), vmem, vmem, pl.BlockSpec(memory_space=pltpu.HBM)] + [vmem] * len(heads),
+        out_specs=(vmem,) * (2 + more),
         scratch_shapes=[
             pltpu.VMEM((ABD, max(start_of(q0 + nq - 1) + SPAN - start_of(q0 + 2), 128)), F32),
-            pltpu.VMEM((2 * ABP, SPAN), BF),
-            pltpu.VMEM((2 * ABP, SPAN), BF),
+            pltpu.VMEM((ABS, SPAN), BF),
+            pltpu.VMEM((ABS, SPAN), BF),
             pltpu.VMEM((5, 512, WIN), BF),
             pltpu.VMEM((5, 512, WIN), BF),
             pltpu.SemaphoreType.DMA((nq // 2,)),
-        ],
+        ]
+        + [pltpu.VMEM((ABD, HEAD), F32), pltpu.SemaphoreType.DMA((2,))] * (not q0),
         compiler_params=pltpu.CompilerParams(vmem_limit_bytes=SORT_VMEM),
-        cost_estimate=pl.CostEstimate(flops=nq * 5 * 2 * 320 * 512 * 512, bytes_accessed=nq * 1300000, transcendentals=0),
+        cost_estimate=pl.CostEstimate(flops=nq * 5 * 2 * ABS * 512 * 512, bytes_accessed=nq * 1300000, transcendentals=0),
         name="sort_ints",
-    )(virt, aux, tail, head, in_hbm(ints))
+    )(virt, aux, tail, in_hbm(ints), *heads)
 
 
 def contract(rows, pieces, parts):
     widths = tuple(p[0].shape[2] for p in parts)
-    flat = [x for p in parts for x in p[:2]]
+    flat = [p[0] for p in parts]
     vmem = pl.BlockSpec(memory_space=pltpu.VMEM)
     hbm = pl.BlockSpec(memory_space=pl.ANY)
     return pl.pallas_call(
@@ -366,14 +373,14 @@
         scratch_shapes=[
             pltpu.VMEM((OP, PAY), BF),
             pltpu.VMEM((OP, PAY), BF),
-            pltpu.VMEM((ABP, OP), F32),
+            pltpu.VMEM((ABD, OP), F32),
             pltpu.VMEM((8, OP), F32),
             pltpu.VMEM((OP, ABP), F32),
         ],
         compiler_params=pltpu.CompilerParams(vmem_limit_bytes=VMEM_LIMIT),
         cost_estimate=pl.CostEstimate(flops=3 * 2 * 1280 * 2560 * 256, bytes_accessed=16000000, transcendentals=0),
         name="contract",
-    )(*pieces, *[pltpu.with_memory_space_constraint(x, pltpu.VMEM) for x in flat], *[p[2] for p in parts])
+    )(*pieces, *[pltpu.with_memory_space_constraint(x, pltpu.VMEM) for x in flat], *[p[1] for p in parts])
 
 
 def at(x, y, core):
@@ -397,22 +404,22 @@
 def body(amplitudes, pair_irrep, virt_irrep, resid_in, ladder_ints):
     blk = functools.partial(lax.axis_index, "blk")
     hold = lax.optimization_barrier
-    pay, four, aux, tail, head = compact(blk, virt_irrep, pair_irrep, amplitudes, ladder_ints)
-
-    def sort(q0, nq, aux, head):
+    pay, four, aux, tail = compact(blk, virt_irrep, pair_irrep, amplitudes, ladder_ints)
+
+    def sort(q0, nq, aux, head=None):
         return list(sort_part(blk, q0, nq, virt_irrep, aux, tail, head, ladder_ints))
 
     line = [lax.ppermute(pay, "rows", walk(h, False)) for h in HOPS[1:]]
-    parts = [sort(*PARTS[0], aux, head)]
-    line, parts[0][2], aux = hold((line, parts[0][2], aux))
+    parts = [sort(*PARTS[0], aux)]
+    line, parts[0][1], aux = hold((line, parts[0][1], aux))
     for i, x in enumerate(line):
         four = lax.dynamic_update_slice(four, x, (OJ * (i + 1), 0))
     near = [lax.ppermute(four, "rows", walk(h, True)) for h in HOPS[1:]]
     far = [lax.ppermute(four, "rows", SWAP)]
-    parts.append(sort(*PARTS[1], aux, parts[0][3]))
-    near, parts[1][2], aux = hold((near, parts[1][2], aux))
+    parts.append(sort(*PARTS[1], aux, parts[0][2]))
+    near, parts[1][1], aux = hold((near, parts[1][1], aux))
     far += [lax.ppermute(p, "rows", SWAP) for p in near]
-    parts.append(sort(*PARTS[2], aux, parts[1][3]))
+    parts.append(sort(*PARTS[2], aux, parts[1][2]))
     terms = contract(functools.partial(lax.axis_index, "rows"), [four] + near + far, parts)
     return finish(lax.all_to_all(terms, "blk", 0, 0), resid_in)
 

time: 57.7 us -> 55.7 us (0.965); the launches traced: 57.5 us -> 54.7 us
  waiting for transfers between devices: 3 us -> 1.25 us
  Pallas kernels: 24.1 us -> 23.1 us
    ppermute x3, waiting for transfers between devices: 2.98 us -> 1.23 us  [body(): line = [lax.ppermute(pay, 'rows', walk(h, False)) for h in HOPS[1:]]]
    pallas_call x1, Pallas kernels: 3.79 us -> 2.56 us  [compact(): pl.pallas_call(functools.partial(compact_kernel, blk), out_shape=(pltpu.V...]
  transfers between devices with their start and end apart: 10 -> 10, of which waited for: 2 -> 1; matrix products, arithmetic and copies ran while one was open for 0% -> 0% of each run, Pallas kernels for 24% -> 26%
where the time goes in v4:
time: 55.7 us; the launch traced here: 54.7 us
  Pallas kernels  23.1 us (41%)
  blocking collectives  18.3 us (33%)
  starting transfers between devices  11.2 us (20%)
  waiting for transfers between devices  1.25 us (2%)
  other arithmetic  0.64 us (1%)
    all_to_all x1, blocking collectives, body(): return finish(lax.all_to_all(terms, 'blk', 0, 0), resid_in)  18.3 us
    pallas_call x3, Pallas kernels, sort_part(): pl.pallas_call(functools.partial(sort_kernel, blk, q0, nq), out_shape=(sh...  14.2 us
    ppermute x3, starting transfers between devices, body(): near = [lax.ppermute(four, 'rows', walk(h, True)) for h in HOPS[1:]]  6.52 us
    pallas_call x1, Pallas kernels, contract(): pl.pallas_call(functools.partial(main_kernel, rows, widths), out_shape=ja...  6.36 us
    ppermute x3, starting transfers between devices, body(): line = [lax.ppermute(pay, 'rows', walk(h, False)) for h in HOPS[1:]]  3.59 us
    pallas_call x1, Pallas kernels, compact(): pl.pallas_call(functools.partial(compact_kernel, blk), out_shape=(pltpu.V...  2.56 us
    ppermute x3, waiting for transfers between devices, body(): line = [lax.ppermute(pay, 'rows', walk(h, False)) for h in HOPS[1:]]  1.23 us
  transfers between devices with their start and end apart: 10, of which 1 were waited for; matrix products, arithmetic and copies ran while one was open for 0% of the time, Pallas kernels for 26%

profile of v4, /device:TPU:6, one launch (start us, length us, event | category | flops | bytes accessed | tf_op | source)
XLA Modules:
  0.0 54.7 jit_solution(13211660423082788600)
XLA Ops:
  0.0 0.0 copy-start
  0.0 2.6 %compact.1 = (f32[8,2560]{1,0:T(8,128)S(1)}, f32[32,2560]{1,0:T(8,128)S(1)}, s32[8,16,512]{2,1,0:T(8,128)S(1)}, f32[152,128]{1,0:T(8,128)S(1)}) custom-call(s32[400]{0:T(512)} %virt_s.7, s32[8]{0:T(128)} %pair_s.1, s32[1,400]{1,0:T(1,128)} %bitcast.1, f32[8,20000]{1,0:T(8,128)} %amp.1, f32[152,20000]{1,0:T(8,128)} %ints.5), custom_call_target="tpu_custom_call" | custom-call | tf_op jit(solution)/shard_map/compact/pallas_call | solution.py:310
  2.6 1.5 %collective-permute-start = (f32[8,2560]{1,0:T(8,128)S(1)}, f32[8,2560]{1,0:T(8,128)S(1)}, u32[]{:S(2)}, u32[]{:S(2)}) collective-permute-start(f32[8,2560]{1,0:T(8,128)S(1)} %get-tuple-element.28), channel_id=1, source_target_pairs={{0,128},{8,40},{16,144},{24,56},{32,160},{40,8},{48,176},{56,24},{... | collective-permute-start | bytes 245768 | tf_op jit(solution)/shard_map/ppermute | solution.py:412
  4.1 2.1 %collective-permute-start.1 = (f32[8,2560]{1,0:T(8,128)S(1)}, f32[8,2560]{1,0:T(8,128)S(1)}, u32[]{:S(2)}, u32[]{:S(2)}) collective-permute-start(f32[8,2560]{1,0:T(8,128)S(1)} %get-tuple-element.28), channel_id=1, source_target_pairs={{0,64},{8,24},{16,80},{24,40},{32,96},{40,56},{48,112},{56,8},{64,... | collective-permute-start | bytes 245768 | tf_op jit(solution)/shard_map/ppermute | solution.py:412
  6.2 0.0 collective-permute-start.2
  6.2 0.0 copy-done
  6.2 4.4 %sort_ints.3 = (bf16[8,304,512]{2,1,0:T(8,128)(2,1)S(1)}, f32[8,128]{1,0:T(8,128)S(1)}, f32[152,4224]{1,0:T(8,128)S(1)}) custom-call(s32[400]{0:T(512)S(1)} %copy-done, s32[8,16,512]{2,1,0:T(8,128)S(1)} %get-tuple-element.43.aux, f32[152,128]{1,0:T(8,128)S(1)} %get-tuple-element.30.tail, f32[152,20000]{1,0:T(8,128)} %ints.5), custom_call_target="tpu_custom_call" | custom-call | flops 1593835520 | bytes 2600000 | tf_op jit(solution)/shard_map/sort_ints/pallas_call | solution.py:343
  10.6 0.0 collective-permute-done
  10.6 0.0 collective-permute-done.1
  10.6 1.2 %collective-permute-done.2 = f32[8,2560]{1,0:T(8,128)S(1)} collective-permute-done((f32[8,2560]{1,0:T(8,128)S(1)}, f32[8,2560]{1,0:T(8,128)S(1)}, u32[]{:S(2)}, u32[]{:S(2)}) %collective-permute-start.2) | collective-permute-done | bytes 81952 | tf_op jit(solution)/shard_map/ppermute | solution.py:412
  11.8 3.3 %collective-permute-start.3 = (f32[32,2560]{1,0:T(8,128)S(1)}, f32[32,2560]{1,0:T(8,128)S(1)}, u32[]{:S(2)}, u32[]{:S(2)}) collective-permute-start(f32[32,2560]{1,0:T(8,128)S(1)} %constant_dynamic-update-slice_fusion.refs_0_), channel_id=1, source_target_pairs={{0,32},{8,136},{16,48},{24,152},{32,0},{40,168},{48,16},{56,184},{... | collective-permute-start | bytes 983048 | tf_op jit(solution)/shard_map/ppermute | solution.py:417
  15.1 0.7 %collective-permute-start.4 = (f32[32,2560]{1,0:T(8,128)S(1)}, f32[32,2560]{1,0:T(8,128)S(1)}, u32[]{:S(2)}, u32[]{:S(2)}) collective-permute-start(f32[32,2560]{1,0:T(8,128)S(1)} %constant_dynamic-update-slice_fusion.refs_0_), channel_id=1, source_target_pairs={{0,16},{8,72},{16,32},{24,88},{32,48},{40,104},{48,0},{56,120},{64... | collective-permute-start | bytes 983048 | tf_op jit(solution)/shard_map/ppermute | solution.py:417
  15.8 2.6 %collective-permute-start.5 = (f32[32,2560]{1,0:T(8,128)S(1)}, f32[32,2560]{1,0:T(8,128)S(1)}, u32[]{:S(2)}, u32[]{:S(2)}) collective-permute-start(f32[32,2560]{1,0:T(8,128)S(1)} %constant_dynamic-update-slice_fusion.refs_0_), channel_id=1, source_target_pairs={{0,48},{8,200},{16,0},{24,216},{32,16},{40,232},{48,32},{56,248},{... | collective-permute-start | bytes 983048 | tf_op jit(solution)/shard_map/ppermute | solution.py:417
  18.4 0.0 collective-permute-start.6
  18.4 7.1 %sort_ints.4 = (bf16[8,304,1536]{2,1,0:T(8,128)(2,1)S(1)}, f32[8,128]{1,0:T(8,128)S(1)}, f32[152,4224]{1,0:T(8,128)S(1)}) custom-call(s32[400]{0:T(512)S(1)} %copy-done, s32[8,16,512]{2,1,0:T(8,128)S(1)} %get-tuple-element.43.aux, f32[152,128]{1,0:T(8,128)S(1)} %get-tuple-element.30.tail, f32[152,20000]{1,0:T(8,128)} %ints.5, ...), custom_call_target="tpu_custom_call" | custom-call | flops 4781506560 | bytes 7800000 | tf_op jit(solution)/shard_map/sort_ints/pallas_call | solution.py:343
  25.5 0.0 collective-permute-done.3.refs_1_
  25.5 0.0 collective-permute-done.4.refs_2_
  25.5 0.0 collective-permute-done.5.refs_3_
  25.5 0.6 %collective-permute-start.7 = (f32[32,2560]{1,0:T(8,128)S(1)}, f32[32,2560]{1,0:T(8,128)S(1)}, u32[]{:S(2)}, u32[]{:S(2)}) collective-permute-start(f32[32,2560]{1,0:T(8,128)S(1)} %collective-permute-done.3.refs_1_), channel_id=1, source_target_pairs={{0,8},{8,0},{16,24},{24,16},{32,40},{40,32},{48,56},{56,48},{64,72... | collective-permute-start | bytes 983048 | tf_op jit(solution)/shard_map/ppermute | solution.py:421
  26.1 0.1 collective-permute-start.8
  26.2 0.4 collective-permute-start.9
  26.6 2.7 %sort_ints.5 = (bf16[8,304,512]{2,1,0:T(8,128)(2,1)S(1)}, f32[8,128]{1,0:T(8,128)S(1)}) custom-call(s32[400]{0:T(512)S(1)} %copy-done, s32[8,16,512]{2,1,0:T(8,128)S(1)} %get-tuple-element.43.aux, f32[152,128]{1,0:T(8,128)S(1)} %get-tuple-element.30.tail, f32[152,20000]{1,0:T(8,128)} %ints.5, f32[152,4224]{1,0:T(8,128)S(1)} %get-tuple-element.44.refs_0_), custom_call_target="tpu_custom_call" | custom-call | flops 1593835520 | bytes 2600000 | tf_op jit(solution)/shard_map/sort_ints/pallas_call | solution.py:343
  29.3 0.0 collective-permute-done.6.refs_4_
  29.3 0.0 collective-permute-done.7.refs_5_
  29.3 0.0 collective-permute-done.8.refs_6_
  29.3 0.0 collective-permute-done.9.refs_7_
  29.3 0.0 copy-start.1
  29.4 6.4 %contract.1 = f32[8,40,128]{2,1,0:T(8,128)S(1)} custom-call(f32[32,2560]{1,0:T(8,128)S(1)} %constant_dynamic-update-slice_fusion.refs_0_, f32[32,2560]{1,0:T(8,128)S(1)} %collective-permute-done.3.refs_1_, f32[32,2560]{1,0:T(8,128)S(1)} %collective-permute-done.4.refs_2_, f32[32,2560]{1,0:T(8,128)S(1)} %collective-permute-done.5.refs_3_, ...), custom_call_target="tpu_custom_call" | custom-call | flops 5033164800 | bytes 16000000 | tf_op jit(solution)/shard_map/contract/pallas_call | solution.py:368
  35.7 18.3 %all_to_all.5 = f32[8,40,128]{2,1,0:T(8,128)S(1)} all-to-all(f32[8,40,128]{2,1,0:T(8,128)S(1)} %contract.1), channel_id=1, replica_groups=mesh['rows'=32,'blk'=8] {'blk'}, dimensions={0} | all-to-all | bytes 327680 | tf_op jit(solution)/shard_map/all_to_all | solution.py:424
  54.0 0.1 fusion
  54.1 0.0 copy-done.1
  54.1 0.6 %maximum_add_fusion = f32[32,152]{1,0:T(8,128)} fusion(f32[32,152]{1,0:T(8,128)S(1)} %copy-done.1, f32[8,24]{1,0:T(8,128)S(1)} %get-tuple-element.50, f32[8,24]{1,0:T(8,128)S(1)} %get-tuple-element.51, f32[8,24]{1,0:T(8,128)S(1)} %get-tuple-element.52, f32[8,24]{1,0:T(8,128)S(1)} %get-tuple-element.49, f32[32,128]{1,0:T(8,128)S(1)} %slice.20), kind=kLoop, calls=%fused_computation | loop fusion | flops 24320 | bytes 58368 | tf_op jit(solution)/shard_map/add | solution.py:294
  (5 shorter events, 0.0 us)
Async XLA Ops:
  0.0 6.2 %copy-start = (s32[400]{0:T(512)S(1)}, s32[400]{0:T(512)}, u32[]{:S(2)}) copy-start(s32[400]{0:T(512)} %virt_s.7) | copy-start | bytes 4804
  2.6 8.0 %collective-permute-start = (f32[8,2560]{1,0:T(8,128)S(1)}, f32[8,2560]{1,0:T(8,128)S(1)}, u32[]{:S(2)}, u32[]{:S(2)}) collective-permute-start(f32[8,2560]{1,0:T(8,128)S(1)} %get-tuple-element.28), channel_id=1, source_target_pairs={{0,128},{8,40},{16,144},{24,56},{32,160},{40,8},{48,176},{56,24},{... | collective-permute-start | bytes 245768 | tf_op jit(solution)/shard_map/ppermute | solution.py:412
  4.1 6.5 %collective-permute-start.1 = (f32[8,2560]{1,0:T(8,128)S(1)}, f32[8,2560]{1,0:T(8,128)S(1)}, u32[]{:S(2)}, u32[]{:S(2)}) collective-permute-start(f32[8,2560]{1,0:T(8,128)S(1)} %get-tuple-element.28), channel_id=1, source_target_pairs={{0,64},{8,24},{16,80},{24,40},{32,96},{40,56},{48,112},{56,8},{64,... | collective-permute-start | bytes 245768 | tf_op jit(solution)/shard_map/ppermute | solution.py:412
  6.2 5.7 %collective-permute-start.2 = (f32[8,2560]{1,0:T(8,128)S(1)}, f32[8,2560]{1,0:T(8,128)S(1)}, u32[]{:S(2)}, u32[]{:S(2)}) collective-permute-start(f32[8,2560]{1,0:T(8,128)S(1)} %get-tuple-element.28), channel_id=1, source_target_pairs={{0,192},{8,56},{16,208},{24,8},{32,224},{40,24},{48,240},{56,40},{... | collective-permute-start | bytes 245768 | tf_op jit(solution)/shard_map/ppermute | solution.py:412
  11.8 13.6 %collective-permute-start.3 = (f32[32,2560]{1,0:T(8,128)S(1)}, f32[32,2560]{1,0:T(8,128)S(1)}, u32[]{:S(2)}, u32[]{:S(2)}) collective-permute-start(f32[32,2560]{1,0:T(8,128)S(1)} %constant_dynamic-update-slice_fusion.refs_0_), channel_id=1, source_target_pairs={{0,32},{8,136},{16,48},{24,152},{32,0},{40,168},{48,16},{56,184},{... | collective-permute-start | bytes 983048 | tf_op jit(solution)/shard_map/ppermute | solution.py:417
  15.1 10.4 %collective-permute-start.4 = (f32[32,2560]{1,0:T(8,128)S(1)}, f32[32,2560]{1,0:T(8,128)S(1)}, u32[]{:S(2)}, u32[]{:S(2)}) collective-permute-start(f32[32,2560]{1,0:T(8,128)S(1)} %constant_dynamic-update-slice_fusion.refs_0_), channel_id=1, source_target_pairs={{0,16},{8,72},{16,32},{24,88},{32,48},{40,104},{48,0},{56,120},{64... | collective-permute-start | bytes 983048 | tf_op jit(solution)/shard_map/ppermute | solution.py:417
  15.8 9.7 %collective-permute-start.5 = (f32[32,2560]{1,0:T(8,128)S(1)}, f32[32,2560]{1,0:T(8,128)S(1)}, u32[]{:S(2)}, u32[]{:S(2)}) collective-permute-start(f32[32,2560]{1,0:T(8,128)S(1)} %constant_dynamic-update-slice_fusion.refs_0_), channel_id=1, source_target_pairs={{0,48},{8,200},{16,0},{24,216},{32,16},{40,232},{48,32},{56,248},{... | collective-permute-start | bytes 983048 | tf_op jit(solution)/shard_map/ppermute | solution.py:417
  18.4 10.9 %collective-permute-start.6 = (f32[32,2560]{1,0:T(8,128)S(1)}, f32[32,2560]{1,0:T(8,128)S(1)}, u32[]{:S(2)}, u32[]{:S(2)}) collective-permute-start(f32[32,2560]{1,0:T(8,128)S(1)} %constant_dynamic-update-slice_fusion.refs_0_), channel_id=1, source_target_pairs={{0,8},{8,0},{16,24},{24,16},{32,40},{40,32},{48,56},{56,48},{64,72... | collective-permute-start | bytes 983048 | tf_op jit(solution)/shard_map/ppermute | solution.py:418
  25.5 3.8 %collective-permute-start.7 = (f32[32,2560]{1,0:T(8,128)S(1)}, f32[32,2560]{1,0:T(8,128)S(1)}, u32[]{:S(2)}, u32[]{:S(2)}) collective-permute-start(f32[32,2560]{1,0:T(8,128)S(1)} %collective-permute-done.3.refs_1_), channel_id=1, source_target_pairs={{0,8},{8,0},{16,24},{24,16},{32,40},{40,32},{48,56},{56,48},{64,72... | collective-permute-start | bytes 983048 | tf_op jit(solution)/shard_map/ppermute | solution.py:421
  26.1 3.3 %collective-permute-start.8 = (f32[32,2560]{1,0:T(8,128)S(1)}, f32[32,2560]{1,0:T(8,128)S(1)}, u32[]{:S(2)}, u32[]{:S(2)}) collective-permute-start(f32[32,2560]{1,0:T(8,128)S(1)} %collective-permute-done.4.refs_2_), channel_id=1, source_target_pairs={{0,8},{8,0},{16,24},{24,16},{32,40},{40,32},{48,56},{56,48},{64,72... | collective-permute-start | bytes 983048 | tf_op jit(solution)/shard_map/ppermute | solution.py:421
  26.2 3.2 %collective-permute-start.9 = (f32[32,2560]{1,0:T(8,128)S(1)}, f32[32,2560]{1,0:T(8,128)S(1)}, u32[]{:S(2)}, u32[]{:S(2)}) collective-permute-start(f32[32,2560]{1,0:T(8,128)S(1)} %collective-permute-done.5.refs_3_), channel_id=1, source_target_pairs={{0,8},{8,0},{16,24},{24,16},{32,40},{40,32},{48,56},{56,48},{64,72... | collective-permute-start | bytes 983048 | tf_op jit(solution)/shard_map/ppermute | solution.py:421
  29.3 24.8 %copy-start.1 = (f32[32,152]{1,0:T(8,128)S(1)}, f32[32,152]{1,0:T(8,128)}, u32[]{:S(2)}) copy-start(f32[32,152]{1,0:T(8,128)} %param.8) | copy-start | bytes 58372

commit v5 on v4

--- a/solution.py
+++ b/solution.py
@@ -29,7 +29,7 @@
 EDGE = CD // 128 * 128
 HOPS = (0, 2, 1, 3)
 PARTS = ((0, 2), (2, 6), (8, 2))
-SECT = 4
+SECT = 8
 VMEM_LIMIT = 24 * 1024 * 1024
 COMPACT_VMEM = 56 * 1024 * 1024
 SORT_VMEM = 22 * 1024 * 1024
@@ -177,10 +177,7 @@
         hi = w.astype(BF).astype(F32)
         b[...] = jnp.concatenate([hi, w - hi], axis=0).astype(BF)
 
-    def sort(i, e, b, m):
-        start = NV * 5 * (q0 + i)
-        at = start - start // 128 * 128 + NV * e
-        first = at // 128 * 128
+    def build(i, e, m):
         v = (5 * (q0 + i) + e) % 8
         rank = aux[v, 0:8, :]
         irrep = aux[v, 8:16, :]
@@ -196,6 +193,12 @@
         for u in range(4):
             on = jnp.where(half[0:1, :] == u, 1.0, 0.0).astype(BF)
             m[e, 128 * u : 128 * u + 128, :] = pick * jnp.broadcast_to(on, (128, WIN))
+
+    def sort(i, e, b, m, built=False):
+        if not built:
+            build(i, e, m)
+        at = NV * 5 * (q0 + i) - start_of(q0 + i) + NV * e
+        first = at // 128 * 128
         return nt(b[:, first : first + WIN], m[e]).astype(BF)
 
     def merge(i, u, parts):
@@ -213,19 +216,22 @@
         if k:
             copies[k - 1].wait()
         if first and not k:
+            for e in range(5):
+                build(i, e, ma)
+                build(i + 1, e, mb)
             first[0].wait()
             load(i, ba)
-            pa = [sort(i, e, ba, ma) for e in range(2)]
+            pa = [sort(i, e, ba, ma, True) for e in range(2)]
             first[1].wait()
             load(i + 1, bb)
-            pa += [sort(i, e, ba, ma) for e in range(2, 5)]
+            pa += [sort(i, e, ba, ma, True) for e in range(2, 5)]
         else:
             load(i, ba)
             load(i + 1, bb)
             pa = [sort(i, e, ba, ma) for e in range(5)]
         pb = []
         for e in range(5):
-            pb.append(sort(i + 1, e, bb, mb))
+            pb.append(sort(i + 1, e, bb, mb, bool(first) and not k))
             if e < 4:
                 merge(i, e, pa)
         for u in range(4):

time: 55.7 us -> 55 us (0.987)
  Pallas kernels: 23.1 us -> 22.4 us
    pallas_call x1, Pallas kernels: 6.36 us -> 5.79 us  [contract(): pl.pallas_call(functools.partial(main_kernel, rows, widths), out_shape=ja...]
where the time goes in v5:
time: 55 us; the launch traced here: 54.2 us
  Pallas kernels  22.4 us (41%)
  blocking collectives  18.3 us (33%)
  starting transfers between devices  11.2 us (20%)
  waiting for transfers between devices  1.39 us (3%)
  other arithmetic  0.64 us (1%)
    all_to_all x1, blocking collectives, body(): return finish(lax.all_to_all(terms, 'blk', 0, 0), resid_in)  18.3 us
    pallas_call x3, Pallas kernels, sort_part(): pl.pallas_call(functools.partial(sort_kernel, blk, q0, nq), out_shape=(sh...  14.1 us
    ppermute x3, starting transfers between devices, body(): near = [lax.ppermute(four, 'rows', walk(h, True)) for h in HOPS[1:]]  6.52 us
    pallas_call x1, Pallas kernels, contract(): pl.pallas_call(functools.partial(main_kernel, rows, widths), out_shape=ja...  5.79 us
    ppermute x3, starting transfers between devices, body(): line = [lax.ppermute(pay, 'rows', walk(h, False)) for h in HOPS[1:]]  3.59 us
    pallas_call x1, Pallas kernels, compact(): pl.pallas_call(functools.partial(compact_kernel, blk), out_shape=(pltpu.V...  2.56 us
    ppermute x3, waiting for transfers between devices, body(): line = [lax.ppermute(pay, 'rows', walk(h, False)) for h in HOPS[1:]]  1.38 us
  transfers between devices with their start and end apart: 10, of which 1 were waited for; matrix products, arithmetic and copies ran while one was open for 0% of the time, Pallas kernels for 26%

profile of v5, /device:TPU:6, one launch (start us, length us, event | category | flops | bytes accessed | tf_op | source)
XLA Modules:
  0.0 54.2 jit_solution(818698355766650846)
XLA Ops:
  0.0 0.0 copy-start
  0.0 2.6 %compact.1 = (f32[8,2560]{1,0:T(8,128)S(1)}, f32[32,2560]{1,0:T(8,128)S(1)}, s32[8,16,512]{2,1,0:T(8,128)S(1)}, f32[152,128]{1,0:T(8,128)S(1)}) custom-call(s32[400]{0:T(512)} %virt_s.7, s32[8]{0:T(128)} %pair_s.1, s32[1,400]{1,0:T(1,128)} %bitcast.1, f32[8,20000]{1,0:T(8,128)} %amp.1, f32[152,20000]{1,0:T(8,128)} %ints.5), custom_call_target="tpu_custom_call" | custom-call | tf_op jit(solution)/shard_map/compact/pallas_call | solution.py:316
  2.6 1.5 %collective-permute-start = (f32[8,2560]{1,0:T(8,128)S(1)}, f32[8,2560]{1,0:T(8,128)S(1)}, u32[]{:S(2)}, u32[]{:S(2)}) collective-permute-start(f32[8,2560]{1,0:T(8,128)S(1)} %get-tuple-element.28), channel_id=1, source_target_pairs={{0,128},{8,40},{16,144},{24,56},{32,160},{40,8},{48,176},{56,24},{... | collective-permute-start | bytes 245768 | tf_op jit(solution)/shard_map/ppermute | solution.py:418
  4.1 2.1 %collective-permute-start.1 = (f32[8,2560]{1,0:T(8,128)S(1)}, f32[8,2560]{1,0:T(8,128)S(1)}, u32[]{:S(2)}, u32[]{:S(2)}) collective-permute-start(f32[8,2560]{1,0:T(8,128)S(1)} %get-tuple-element.28), channel_id=1, source_target_pairs={{0,64},{8,24},{16,80},{24,40},{32,96},{40,56},{48,112},{56,8},{64,... | collective-permute-start | bytes 245768 | tf_op jit(solution)/shard_map/ppermute | solution.py:418
  6.2 0.0 collective-permute-start.2
  6.2 0.0 copy-done
  6.2 4.2 %sort_ints.3 = (bf16[8,304,512]{2,1,0:T(8,128)(2,1)S(1)}, f32[8,128]{1,0:T(8,128)S(1)}, f32[152,4224]{1,0:T(8,128)S(1)}) custom-call(s32[400]{0:T(512)S(1)} %copy-done, s32[8,16,512]{2,1,0:T(8,128)S(1)} %get-tuple-element.43.aux, f32[152,128]{1,0:T(8,128)S(1)} %get-tuple-element.30.tail, f32[152,20000]{1,0:T(8,128)} %ints.5), custom_call_target="tpu_custom_call" | custom-call | flops 1593835520 | bytes 2600000 | tf_op jit(solution)/shard_map/sort_ints/pallas_call | solution.py:349
  10.4 0.0 collective-permute-done
  10.4 0.0 collective-permute-done.1
  10.4 1.4 %collective-permute-done.2 = f32[8,2560]{1,0:T(8,128)S(1)} collective-permute-done((f32[8,2560]{1,0:T(8,128)S(1)}, f32[8,2560]{1,0:T(8,128)S(1)}, u32[]{:S(2)}, u32[]{:S(2)}) %collective-permute-start.2) | collective-permute-done | bytes 81952 | tf_op jit(solution)/shard_map/ppermute | solution.py:418
  11.8 3.3 %collective-permute-start.3 = (f32[32,2560]{1,0:T(8,128)S(1)}, f32[32,2560]{1,0:T(8,128)S(1)}, u32[]{:S(2)}, u32[]{:S(2)}) collective-permute-start(f32[32,2560]{1,0:T(8,128)S(1)} %constant_dynamic-update-slice_fusion.refs_0_), channel_id=1, source_target_pairs={{0,32},{8,136},{16,48},{24,152},{32,0},{40,168},{48,16},{56,184},{... | collective-permute-start | bytes 983048 | tf_op jit(solution)/shard_map/ppermute | solution.py:423
  15.1 0.7 %collective-permute-start.4 = (f32[32,2560]{1,0:T(8,128)S(1)}, f32[32,2560]{1,0:T(8,128)S(1)}, u32[]{:S(2)}, u32[]{:S(2)}) collective-permute-start(f32[32,2560]{1,0:T(8,128)S(1)} %constant_dynamic-update-slice_fusion.refs_0_), channel_id=1, source_target_pairs={{0,16},{8,72},{16,32},{24,88},{32,48},{40,104},{48,0},{56,120},{64... | collective-permute-start | bytes 983048 | tf_op jit(solution)/shard_map/ppermute | solution.py:423
  15.8 2.6 %collective-permute-start.5 = (f32[32,2560]{1,0:T(8,128)S(1)}, f32[32,2560]{1,0:T(8,128)S(1)}, u32[]{:S(2)}, u32[]{:S(2)}) collective-permute-start(f32[32,2560]{1,0:T(8,128)S(1)} %constant_dynamic-update-slice_fusion.refs_0_), channel_id=1, source_target_pairs={{0,48},{8,200},{16,0},{24,216},{32,16},{40,232},{48,32},{56,248},{... | collective-permute-start | bytes 983048 | tf_op jit(solution)/shard_map/ppermute | solution.py:423
  18.4 0.0 collective-permute-start.6
  18.4 7.1 %sort_ints.4 = (bf16[8,304,1536]{2,1,0:T(8,128)(2,1)S(1)}, f32[8,128]{1,0:T(8,128)S(1)}, f32[152,4224]{1,0:T(8,128)S(1)}) custom-call(s32[400]{0:T(512)S(1)} %copy-done, s32[8,16,512]{2,1,0:T(8,128)S(1)} %get-tuple-element.43.aux, f32[152,128]{1,0:T(8,128)S(1)} %get-tuple-element.30.tail, f32[152,20000]{1,0:T(8,128)} %ints.5, ...), custom_call_target="tpu_custom_call" | custom-call | flops 4781506560 | bytes 7800000 | tf_op jit(solution)/shard_map/sort_ints/pallas_call | solution.py:349
  25.5 0.0 collective-permute-done.3.refs_1_
  25.5 0.0 collective-permute-done.4.refs_2_
  25.5 0.0 collective-permute-done.5.refs_3_
  25.5 0.6 %collective-permute-start.7 = (f32[32,2560]{1,0:T(8,128)S(1)}, f32[32,2560]{1,0:T(8,128)S(1)}, u32[]{:S(2)}, u32[]{:S(2)}) collective-permute-start(f32[32,2560]{1,0:T(8,128)S(1)} %collective-permute-done.3.refs_1_), channel_id=1, source_target_pairs={{0,8},{8,0},{16,24},{24,16},{32,40},{40,32},{48,56},{56,48},{64,72... | collective-permute-start | bytes 983048 | tf_op jit(solution)/shard_map/ppermute | solution.py:427
  26.1 0.1 collective-permute-start.8
  26.2 0.4 collective-permute-start.9
  26.6 2.7 %sort_ints.5 = (bf16[8,304,512]{2,1,0:T(8,128)(2,1)S(1)}, f32[8,128]{1,0:T(8,128)S(1)}) custom-call(s32[400]{0:T(512)S(1)} %copy-done, s32[8,16,512]{2,1,0:T(8,128)S(1)} %get-tuple-element.43.aux, f32[152,128]{1,0:T(8,128)S(1)} %get-tuple-element.30.tail, f32[152,20000]{1,0:T(8,128)} %ints.5, f32[152,4224]{1,0:T(8,128)S(1)} %get-tuple-element.44.refs_0_), custom_call_target="tpu_custom_call" | custom-call | flops 1593835520 | bytes 2600000 | tf_op jit(solution)/shard_map/sort_ints/pallas_call | solution.py:349
  29.3 0.0 collective-permute-done.6.refs_4_
  29.3 0.0 collective-permute-done.7.refs_5_
  29.3 0.0 collective-permute-done.8.refs_6_
  29.3 0.0 collective-permute-done.9.refs_7_
  29.3 0.0 copy-start.1
  29.4 5.8 %contract.1 = f32[8,40,128]{2,1,0:T(8,128)S(1)} custom-call(f32[32,2560]{1,0:T(8,128)S(1)} %constant_dynamic-update-slice_fusion.refs_0_, f32[32,2560]{1,0:T(8,128)S(1)} %collective-permute-done.3.refs_1_, f32[32,2560]{1,0:T(8,128)S(1)} %collective-permute-done.4.refs_2_, f32[32,2560]{1,0:T(8,128)S(1)} %collective-permute-done.5.refs_3_, ...), custom_call_target="tpu_custom_call" | custom-call | flops 5033164800 | bytes 16000000 | tf_op jit(solution)/shard_map/contract/pallas_call | solution.py:374
  35.2 18.3 %all_to_all.5 = f32[8,40,128]{2,1,0:T(8,128)S(1)} all-to-all(f32[8,40,128]{2,1,0:T(8,128)S(1)} %contract.1), channel_id=1, replica_groups=mesh['rows'=32,'blk'=8] {'blk'}, dimensions={0} | all-to-all | bytes 327680 | tf_op jit(solution)/shard_map/all_to_all | solution.py:430
  53.5 0.1 fusion
  53.6 0.0 copy-done.1
  53.6 0.6 %maximum_add_fusion = f32[32,152]{1,0:T(8,128)} fusion(f32[32,152]{1,0:T(8,128)S(1)} %copy-done.1, f32[8,24]{1,0:T(8,128)S(1)} %get-tuple-element.50, f32[8,24]{1,0:T(8,128)S(1)} %get-tuple-element.51, f32[8,24]{1,0:T(8,128)S(1)} %get-tuple-element.52, f32[8,24]{1,0:T(8,128)S(1)} %get-tuple-element.49, f32[32,128]{1,0:T(8,128)S(1)} %slice.20), kind=kLoop, calls=%fused_computation | loop fusion | flops 24320 | bytes 58368 | tf_op jit(solution)/shard_map/add | solution.py:300
  (5 shorter events, 0.0 us)
Async XLA Ops:
  0.0 6.2 %copy-start = (s32[400]{0:T(512)S(1)}, s32[400]{0:T(512)}, u32[]{:S(2)}) copy-start(s32[400]{0:T(512)} %virt_s.7) | copy-start | bytes 4804
  2.6 7.8 %collective-permute-start = (f32[8,2560]{1,0:T(8,128)S(1)}, f32[8,2560]{1,0:T(8,128)S(1)}, u32[]{:S(2)}, u32[]{:S(2)}) collective-permute-start(f32[8,2560]{1,0:T(8,128)S(1)} %get-tuple-element.28), channel_id=1, source_target_pairs={{0,128},{8,40},{16,144},{24,56},{32,160},{40,8},{48,176},{56,24},{... | collective-permute-start | bytes 245768 | tf_op jit(solution)/shard_map/ppermute | solution.py:418
  4.1 6.4 %collective-permute-start.1 = (f32[8,2560]{1,0:T(8,128)S(1)}, f32[8,2560]{1,0:T(8,128)S(1)}, u32[]{:S(2)}, u32[]{:S(2)}) collective-permute-start(f32[8,2560]{1,0:T(8,128)S(1)} %get-tuple-element.28), channel_id=1, source_target_pairs={{0,64},{8,24},{16,80},{24,40},{32,96},{40,56},{48,112},{56,8},{64,... | collective-permute-start | bytes 245768 | tf_op jit(solution)/shard_map/ppermute | solution.py:418
  6.2 5.7 %collective-permute-start.2 = (f32[8,2560]{1,0:T(8,128)S(1)}, f32[8,2560]{1,0:T(8,128)S(1)}, u32[]{:S(2)}, u32[]{:S(2)}) collective-permute-start(f32[8,2560]{1,0:T(8,128)S(1)} %get-tuple-element.28), channel_id=1, source_target_pairs={{0,192},{8,56},{16,208},{24,8},{32,224},{40,24},{48,240},{56,40},{... | collective-permute-start | bytes 245768 | tf_op jit(solution)/shard_map/ppermute | solution.py:418
  11.8 13.6 %collective-permute-start.3 = (f32[32,2560]{1,0:T(8,128)S(1)}, f32[32,2560]{1,0:T(8,128)S(1)}, u32[]{:S(2)}, u32[]{:S(2)}) collective-permute-start(f32[32,2560]{1,0:T(8,128)S(1)} %constant_dynamic-update-slice_fusion.refs_0_), channel_id=1, source_target_pairs={{0,32},{8,136},{16,48},{24,152},{32,0},{40,168},{48,16},{56,184},{... | collective-permute-start | bytes 983048 | tf_op jit(solution)/shard_map/ppermute | solution.py:423
  15.1 10.4 %collective-permute-start.4 = (f32[32,2560]{1,0:T(8,128)S(1)}, f32[32,2560]{1,0:T(8,128)S(1)}, u32[]{:S(2)}, u32[]{:S(2)}) collective-permute-start(f32[32,2560]{1,0:T(8,128)S(1)} %constant_dynamic-update-slice_fusion.refs_0_), channel_id=1, source_target_pairs={{0,16},{8,72},{16,32},{24,88},{32,48},{40,104},{48,0},{56,120},{64... | collective-permute-start | bytes 983048 | tf_op jit(solution)/shard_map/ppermute | solution.py:423
  15.8 9.7 %collective-permute-start.5 = (f32[32,2560]{1,0:T(8,128)S(1)}, f32[32,2560]{1,0:T(8,128)S(1)}, u32[]{:S(2)}, u32[]{:S(2)}) collective-permute-start(f32[32,2560]{1,0:T(8,128)S(1)} %constant_dynamic-update-slice_fusion.refs_0_), channel_id=1, source_target_pairs={{0,48},{8,200},{16,0},{24,216},{32,16},{40,232},{48,32},{56,248},{... | collective-permute-start | bytes 983048 | tf_op jit(solution)/shard_map/ppermute | solution.py:423
  18.4 10.9 %collective-permute-start.6 = (f32[32,2560]{1,0:T(8,128)S(1)}, f32[32,2560]{1,0:T(8,128)S(1)}, u32[]{:S(2)}, u32[]{:S(2)}) collective-permute-start(f32[32,2560]{1,0:T(8,128)S(1)} %constant_dynamic-update-slice_fusion.refs_0_), channel_id=1, source_target_pairs={{0,8},{8,0},{16,24},{24,16},{32,40},{40,32},{48,56},{56,48},{64,72... | collective-permute-start | bytes 983048 | tf_op jit(solution)/shard_map/ppermute | solution.py:424
  25.5 3.8 %collective-permute-start.7 = (f32[32,2560]{1,0:T(8,128)S(1)}, f32[32,2560]{1,0:T(8,128)S(1)}, u32[]{:S(2)}, u32[]{:S(2)}) collective-permute-start(f32[32,2560]{1,0:T(8,128)S(1)} %collective-permute-done.3.refs_1_), channel_id=1, source_target_pairs={{0,8},{8,0},{16,24},{24,16},{32,40},{40,32},{48,56},{56,48},{64,72... | collective-permute-start | bytes 983048 | tf_op jit(solution)/shard_map/ppermute | solution.py:427
  26.1 3.3 %collective-permute-start.8 = (f32[32,2560]{1,0:T(8,128)S(1)}, f32[32,2560]{1,0:T(8,128)S(1)}, u32[]{:S(2)}, u32[]{:S(2)}) collective-permute-start(f32[32,2560]{1,0:T(8,128)S(1)} %collective-permute-done.4.refs_2_), channel_id=1, source_target_pairs={{0,8},{8,0},{16,24},{24,16},{32,40},{40,32},{48,56},{56,48},{64,72... | collective-permute-start | bytes 983048 | tf_op jit(solution)/shard_map/ppermute | solution.py:427
  26.2 3.2 %collective-permute-start.9 = (f32[32,2560]{1,0:T(8,128)S(1)}, f32[32,2560]{1,0:T(8,128)S(1)}, u32[]{:S(2)}, u32[]{:S(2)}) collective-permute-start(f32[32,2560]{1,0:T(8,128)S(1)} %collective-permute-done.5.refs_3_), channel_id=1, source_target_pairs={{0,8},{8,0},{16,24},{24,16},{32,40},{40,32},{48,56},{56,48},{64,72... | collective-permute-start | bytes 983048 | tf_op jit(solution)/shard_map/ppermute | solution.py:427
  29.3 24.2 %copy-start.1 = (f32[32,152]{1,0:T(8,128)S(1)}, f32[32,152]{1,0:T(8,128)}, u32[]{:S(2)}) copy-start(f32[32,152]{1,0:T(8,128)} %param.8) | copy-start | bytes 58372

commit v6 on v5

--- a/solution.py
+++ b/solution.py
@@ -421,10 +421,9 @@
     for i, x in enumerate(line):
         four = lax.dynamic_update_slice(four, x, (OJ * (i + 1), 0))
     near = [lax.ppermute(four, "rows", walk(h, True)) for h in HOPS[1:]]
-    far = [lax.ppermute(four, "rows", SWAP)]
     parts.append(sort(*PARTS[1], aux, parts[0][2]))
-    near, parts[1][1], aux = hold((near, parts[1][1], aux))
-    far += [lax.ppermute(p, "rows", SWAP) for p in near]
+    near, four, parts[1][1], aux = hold((near, four, parts[1][1], aux))
+    far = [lax.ppermute(p, "rows", SWAP) for p in [four] + near]
     parts.append(sort(*PARTS[2], aux, parts[1][2]))
     terms = contract(functools.partial(lax.axis_index, "rows"), [four] + near + far, parts)
     return finish(lax.all_to_all(terms, "blk", 0, 0), resid_in)

time: 55 us -> 55.9 us (1.016)
  waiting for transfers between devices: 1.39 us -> 3.74 us
  starting transfers between devices: 11.2 us -> 10.1 us
    ppermute x3, waiting for transfers between devices: 0.01 us -> 2.5 us  [body(): near = [lax.ppermute(four, 'rows', walk(h, True)) for h in HOPS[1:]]]
    ppermute x3, starting transfers between devices: 6.52 us -> 5.29 us  [body(): near = [lax.ppermute(four, 'rows', walk(h, True)) for h in HOPS[1:]]]
  transfers between devices with their start and end apart: 10 -> 10, of which waited for: 1 -> 2; matrix products, arithmetic and copies ran while one was open for 0% -> 0% of each run, Pallas kernels for 26% -> 25%
where the time goes in v6:
time: 55.9 us; the launch traced here: 55.3 us
  Pallas kernels  22.4 us (40%)
  blocking collectives  18.2 us (33%)
  starting transfers between devices  10.1 us (18%)
  waiting for transfers between devices  3.74 us (7%)
  other arithmetic  0.64 us (1%)
    all_to_all x1, blocking collectives, body(): return finish(lax.all_to_all(terms, 'blk', 0, 0), resid_in)  18.2 us
    pallas_call x3, Pallas kernels, sort_part(): pl.pallas_call(functools.partial(sort_kernel, blk, q0, nq), out_shape=(sh...  14.1 us
    pallas_call x1, Pallas kernels, contract(): pl.pallas_call(functools.partial(main_kernel, rows, widths), out_shape=ja...  5.77 us
    ppermute x3, starting transfers between devices, body(): near = [lax.ppermute(four, 'rows', walk(h, True)) for h in HOPS[1:]]  5.29 us
    ppermute x3, starting transfers between devices, body(): line = [lax.ppermute(pay, 'rows', walk(h, False)) for h in HOPS[1:]]  3.75 us
    pallas_call x1, Pallas kernels, compact(): pl.pallas_call(functools.partial(compact_kernel, blk), out_shape=(pltpu.V...  2.56 us
    ppermute x3, waiting for transfers between devices, body(): near = [lax.ppermute(four, 'rows', walk(h, True)) for h in HOPS[1:]]  2.5 us
    ppermute x3, waiting for transfers between devices, body(): line = [lax.ppermute(pay, 'rows', walk(h, False)) for h in HOPS[1:]]  1.23 us
  transfers between devices with their start and end apart: 10, of which 2 were waited for; matrix products, arithmetic and copies ran while one was open for 0% of the time, Pallas kernels for 25%

profile of v6, /device:TPU:6, one launch (start us, length us, event | category | flops | bytes accessed | tf_op | source)
XLA Modules:
  0.0 55.3 jit_solution(1249757337252755357)
XLA Ops:
  0.0 0.0 copy-start
  0.0 2.6 %compact.1 = (f32[8,2560]{1,0:T(8,128)S(1)}, f32[32,2560]{1,0:T(8,128)S(1)}, s32[8,16,512]{2,1,0:T(8,128)S(1)}, f32[152,128]{1,0:T(8,128)S(1)}) custom-call(s32[400]{0:T(512)} %virt_s.7, s32[8]{0:T(128)} %pair_s.1, s32[1,400]{1,0:T(1,128)} %bitcast.1, f32[8,20000]{1,0:T(8,128)} %amp.1, f32[152,20000]{1,0:T(8,128)} %ints.5), custom_call_target="tpu_custom_call" | custom-call | tf_op jit(solution)/shard_map/compact/pallas_call | solution.py:316
  2.6 0.9 %collective-permute-start.2 = (f32[8,2560]{1,0:T(8,128)S(1)}, f32[8,2560]{1,0:T(8,128)S(1)}, u32[]{:S(2)}, u32[]{:S(2)}) collective-permute-start(f32[8,2560]{1,0:T(8,128)S(1)} %get-tuple-element.29), channel_id=1, source_target_pairs={{0,192},{8,56},{16,208},{24,8},{32,224},{40,24},{48,240},{56,40},{... | collective-permute-start | bytes 245768 | tf_op jit(solution)/shard_map/ppermute | solution.py:418
  3.5 2.4 %collective-permute-start.1 = (f32[8,2560]{1,0:T(8,128)S(1)}, f32[8,2560]{1,0:T(8,128)S(1)}, u32[]{:S(2)}, u32[]{:S(2)}) collective-permute-start(f32[8,2560]{1,0:T(8,128)S(1)} %get-tuple-element.29), channel_id=1, source_target_pairs={{0,64},{8,24},{16,80},{24,40},{32,96},{40,56},{48,112},{56,8},{64,... | collective-permute-start | bytes 245768 | tf_op jit(solution)/shard_map/ppermute | solution.py:418
  5.9 0.4 collective-permute-start
  6.3 0.0 copy-done
  6.3 4.2 %sort_ints.3 = (bf16[8,304,512]{2,1,0:T(8,128)(2,1)S(1)}, f32[8,128]{1,0:T(8,128)S(1)}, f32[152,4224]{1,0:T(8,128)S(1)}) custom-call(s32[400]{0:T(512)S(1)} %copy-done, s32[8,16,512]{2,1,0:T(8,128)S(1)} %get-tuple-element.45.aux, f32[152,128]{1,0:T(8,128)S(1)} %get-tuple-element.31.tail, f32[152,20000]{1,0:T(8,128)} %ints.5), custom_call_target="tpu_custom_call" | custom-call | flops 1593835520 | bytes 2600000 | tf_op jit(solution)/shard_map/sort_ints/pallas_call | solution.py:349
  10.6 0.0 collective-permute-done.2
  10.6 0.0 collective-permute-done.1
  10.6 1.2 %collective-permute-done = f32[8,2560]{1,0:T(8,128)S(1)} collective-permute-done((f32[8,2560]{1,0:T(8,128)S(1)}, f32[8,2560]{1,0:T(8,128)S(1)}, u32[]{:S(2)}, u32[]{:S(2)}) %collective-permute-start) | collective-permute-done | bytes 81952 | tf_op jit(solution)/shard_map/ppermute | solution.py:418
  11.9 3.1 %collective-permute-start.5 = (f32[32,2560]{1,0:T(8,128)S(1)}, f32[32,2560]{1,0:T(8,128)S(1)}, u32[]{:S(2)}, u32[]{:S(2)}) collective-permute-start(f32[32,2560]{1,0:T(8,128)S(1)} %constant_dynamic-update-slice_fusion.refs_0_), channel_id=1, source_target_pairs={{0,48},{8,200},{16,0},{24,216},{32,16},{40,232},{48,32},{56,248},{... | collective-permute-start | bytes 983048 | tf_op jit(solution)/shard_map/ppermute | solution.py:423
  15.0 0.0 collective-permute-start.4
  15.0 2.2 %collective-permute-start.3 = (f32[32,2560]{1,0:T(8,128)S(1)}, f32[32,2560]{1,0:T(8,128)S(1)}, u32[]{:S(2)}, u32[]{:S(2)}) collective-permute-start(f32[32,2560]{1,0:T(8,128)S(1)} %constant_dynamic-update-slice_fusion.refs_0_), channel_id=1, source_target_pairs={{0,32},{8,136},{16,48},{24,152},{32,0},{40,168},{48,16},{56,184},{... | collective-permute-start | bytes 983048 | tf_op jit(solution)/shard_map/ppermute | solution.py:423
  17.2 7.1 %sort_ints.4 = (bf16[8,304,1536]{2,1,0:T(8,128)(2,1)S(1)}, f32[8,128]{1,0:T(8,128)S(1)}, f32[152,4224]{1,0:T(8,128)S(1)}) custom-call(s32[400]{0:T(512)S(1)} %copy-done, s32[8,16,512]{2,1,0:T(8,128)S(1)} %get-tuple-element.45.aux, f32[152,128]{1,0:T(8,128)S(1)} %get-tuple-element.31.tail, f32[152,20000]{1,0:T(8,128)} %ints.5, ...), custom_call_target="tpu_custom_call" | custom-call | flops 4781506560 | bytes 7800000 | tf_op jit(solution)/shard_map/sort_ints/pallas_call | solution.py:349
  24.2 0.0 collective-permute-done.5.refs_3_
  24.3 2.5 %collective-permute-done.4.refs_2_ = f32[32,2560]{1,0:T(8,128)S(1)} collective-permute-done((f32[32,2560]{1,0:T(8,128)S(1)}, f32[32,2560]{1,0:T(8,128)S(1)}, u32[]{:S(2)}, u32[]{:S(2)}) %collective-permute-start.4) | collective-permute-done | bytes 327712 | tf_op jit(solution)/shard_map/ppermute | solution.py:423
  26.8 0.0 collective-permute-done.3.refs_1_
  26.8 0.0 collective-permute-start.6
  26.8 0.5 collective-permute-start.7
  27.3 0.0 collective-permute-start.8
  27.3 0.5 collective-permute-start.9
  27.8 2.7 %sort_ints.5 = (bf16[8,304,512]{2,1,0:T(8,128)(2,1)S(1)}, f32[8,128]{1,0:T(8,128)S(1)}) custom-call(s32[400]{0:T(512)S(1)} %copy-done, s32[8,16,512]{2,1,0:T(8,128)S(1)} %get-tuple-element.45.aux, f32[152,128]{1,0:T(8,128)S(1)} %get-tuple-element.31.tail, f32[152,20000]{1,0:T(8,128)} %ints.5, f32[152,4224]{1,0:T(8,128)S(1)} %get-tuple-element.46.refs_0_), custom_call_target="tpu_custom_call" | custom-call | flops 1593835520 | bytes 2600000 | tf_op jit(solution)/shard_map/sort_ints/pallas_call | solution.py:349
  30.5 0.0 collective-permute-done.6.refs_4_
  30.5 0.0 collective-permute-done.7.refs_5_
  30.5 0.0 collective-permute-done.8.refs_6_
  30.5 0.0 collective-permute-done.9.refs_7_
  30.6 0.0 copy-start.1
  30.6 5.8 %contract.1 = f32[8,40,128]{2,1,0:T(8,128)S(1)} custom-call(f32[32,2560]{1,0:T(8,128)S(1)} %constant_dynamic-update-slice_fusion.refs_0_, f32[32,2560]{1,0:T(8,128)S(1)} %collective-permute-done.3.refs_1_, f32[32,2560]{1,0:T(8,128)S(1)} %collective-permute-done.4.refs_2_, f32[32,2560]{1,0:T(8,128)S(1)} %collective-permute-done.5.refs_3_, ...), custom_call_target="tpu_custom_call" | custom-call | flops 5033164800 | bytes 16000000 | tf_op jit(solution)/shard_map/contract/pallas_call | solution.py:374
  36.3 18.2 %all_to_all.5 = f32[8,40,128]{2,1,0:T(8,128)S(1)} all-to-all(f32[8,40,128]{2,1,0:T(8,128)S(1)} %contract.1), channel_id=1, replica_groups=mesh['rows'=32,'blk'=8] {'blk'}, dimensions={0} | all-to-all | bytes 327680 | tf_op jit(solution)/shard_map/all_to_all | solution.py:429
  54.6 0.1 fusion
  54.7 0.0 copy-done.1
  54.7 0.6 %maximum_add_fusion = f32[32,152]{1,0:T(8,128)} fusion(f32[32,152]{1,0:T(8,128)S(1)} %copy-done.1, f32[8,24]{1,0:T(8,128)S(1)} %get-tuple-element.52, f32[8,24]{1,0:T(8,128)S(1)} %get-tuple-element.53, f32[8,24]{1,0:T(8,128)S(1)} %get-tuple-element.54, f32[8,24]{1,0:T(8,128)S(1)} %get-tuple-element.51, f32[32,128]{1,0:T(8,128)S(1)} %slice.20), kind=kLoop, calls=%fused_computation | loop fusion | flops 24320 | bytes 58368 | tf_op jit(solution)/shard_map/add | solution.py:300
  (5 shorter events, 0.0 us)
Async XLA Ops:
  0.0 6.3 %copy-start = (s32[400]{0:T(512)S(1)}, s32[400]{0:T(512)}, u32[]{:S(2)}) copy-start(s32[400]{0:T(512)} %virt_s.7) | copy-start | bytes 4804
  2.6 8.0 %collective-permute-start.2 = (f32[8,2560]{1,0:T(8,128)S(1)}, f32[8,2560]{1,0:T(8,128)S(1)}, u32[]{:S(2)}, u32[]{:S(2)}) collective-permute-start(f32[8,2560]{1,0:T(8,128)S(1)} %get-tuple-element.29), channel_id=1, source_target_pairs={{0,192},{8,56},{16,208},{24,8},{32,224},{40,24},{48,240},{56,40},{... | collective-permute-start | bytes 245768 | tf_op jit(solution)/shard_map/ppermute | solution.py:418
  3.5 7.1 %collective-permute-start.1 = (f32[8,2560]{1,0:T(8,128)S(1)}, f32[8,2560]{1,0:T(8,128)S(1)}, u32[]{:S(2)}, u32[]{:S(2)}) collective-permute-start(f32[8,2560]{1,0:T(8,128)S(1)} %get-tuple-element.29), channel_id=1, source_target_pairs={{0,64},{8,24},{16,80},{24,40},{32,96},{40,56},{48,112},{56,8},{64,... | collective-permute-start | bytes 245768 | tf_op jit(solution)/shard_map/ppermute | solution.py:418
  5.9 5.9 %collective-permute-start = (f32[8,2560]{1,0:T(8,128)S(1)}, f32[8,2560]{1,0:T(8,128)S(1)}, u32[]{:S(2)}, u32[]{:S(2)}) collective-permute-start(f32[8,2560]{1,0:T(8,128)S(1)} %get-tuple-element.29), channel_id=1, source_target_pairs={{0,128},{8,40},{16,144},{24,56},{32,160},{40,8},{48,176},{56,24},{... | collective-permute-start | bytes 245768 | tf_op jit(solution)/shard_map/ppermute | solution.py:418
  11.9 12.4 %collective-permute-start.5 = (f32[32,2560]{1,0:T(8,128)S(1)}, f32[32,2560]{1,0:T(8,128)S(1)}, u32[]{:S(2)}, u32[]{:S(2)}) collective-permute-start(f32[32,2560]{1,0:T(8,128)S(1)} %constant_dynamic-update-slice_fusion.refs_0_), channel_id=1, source_target_pairs={{0,48},{8,200},{16,0},{24,216},{32,16},{40,232},{48,32},{56,248},{... | collective-permute-start | bytes 983048 | tf_op jit(solution)/shard_map/ppermute | solution.py:423
  15.0 11.8 %collective-permute-start.4 = (f32[32,2560]{1,0:T(8,128)S(1)}, f32[32,2560]{1,0:T(8,128)S(1)}, u32[]{:S(2)}, u32[]{:S(2)}) collective-permute-start(f32[32,2560]{1,0:T(8,128)S(1)} %constant_dynamic-update-slice_fusion.refs_0_), channel_id=1, source_target_pairs={{0,16},{8,72},{16,32},{24,88},{32,48},{40,104},{48,0},{56,120},{64... | collective-permute-start | bytes 983048 | tf_op jit(solution)/shard_map/ppermute | solution.py:423
  15.0 11.8 %collective-permute-start.3 = (f32[32,2560]{1,0:T(8,128)S(1)}, f32[32,2560]{1,0:T(8,128)S(1)}, u32[]{:S(2)}, u32[]{:S(2)}) collective-permute-start(f32[32,2560]{1,0:T(8,128)S(1)} %constant_dynamic-update-slice_fusion.refs_0_), channel_id=1, source_target_pairs={{0,32},{8,136},{16,48},{24,152},{32,0},{40,168},{48,16},{56,184},{... | collective-permute-start | bytes 983048 | tf_op jit(solution)/shard_map/ppermute | solution.py:423
  26.8 3.8 %collective-permute-start.6 = (f32[32,2560]{1,0:T(8,128)S(1)}, f32[32,2560]{1,0:T(8,128)S(1)}, u32[]{:S(2)}, u32[]{:S(2)}) collective-permute-start(f32[32,2560]{1,0:T(8,128)S(1)} %constant_dynamic-update-slice_fusion.refs_0_), channel_id=1, source_target_pairs={{0,8},{8,0},{16,24},{24,16},{32,40},{40,32},{48,56},{56,48},{64,72... | collective-permute-start | bytes 983048 | tf_op jit(solution)/shard_map/ppermute | solution.py:426
  26.8 3.8 %collective-permute-start.7 = (f32[32,2560]{1,0:T(8,128)S(1)}, f32[32,2560]{1,0:T(8,128)S(1)}, u32[]{:S(2)}, u32[]{:S(2)}) collective-permute-start(f32[32,2560]{1,0:T(8,128)S(1)} %collective-permute-done.3.refs_1_), channel_id=1, source_target_pairs={{0,8},{8,0},{16,24},{24,16},{32,40},{40,32},{48,56},{56,48},{64,72... | collective-permute-start | bytes 983048 | tf_op jit(solution)/shard_map/ppermute | solution.py:426
  27.3 3.3 %collective-permute-start.8 = (f32[32,2560]{1,0:T(8,128)S(1)}, f32[32,2560]{1,0:T(8,128)S(1)}, u32[]{:S(2)}, u32[]{:S(2)}) collective-permute-start(f32[32,2560]{1,0:T(8,128)S(1)} %collective-permute-done.4.refs_2_), channel_id=1, source_target_pairs={{0,8},{8,0},{16,24},{24,16},{32,40},{40,32},{48,56},{56,48},{64,72... | collective-permute-start | bytes 983048 | tf_op jit(solution)/shard_map/ppermute | solution.py:426
  27.3 3.3 %collective-permute-start.9 = (f32[32,2560]{1,0:T(8,128)S(1)}, f32[32,2560]{1,0:T(8,128)S(1)}, u32[]{:S(2)}, u32[]{:S(2)}) collective-permute-start(f32[32,2560]{1,0:T(8,128)S(1)} %collective-permute-done.5.refs_3_), channel_id=1, source_target_pairs={{0,8},{8,0},{16,24},{24,16},{32,40},{40,32},{48,56},{56,48},{64,72... | collective-permute-start | bytes 983048 | tf_op jit(solution)/shard_map/ppermute | solution.py:426
  30.6 24.1 %copy-start.1 = (f32[32,152]{1,0:T(8,128)S(1)}, f32[32,152]{1,0:T(8,128)}, u32[]{:S(2)}) copy-start(f32[32,152]{1,0:T(8,128)} %param.8) | copy-start | bytes 58372
